TPU v7x, 256 devices: a whole 4x4x8 slice. The times are simulated.
256 devices in a mesh: row: 16 (over y, z_hi), col: 16 (over x, z_lo, core).
Axes of the slice: x: 4, y: 4, z: 8 (z_hi: 4, z_lo: 2; z = z_hi * 2 + z_lo), core: 2. Of those that a mesh axis runs over, the one named last changes fastest.
Arguments:
- matrix: float32 [12288, 12288], P('row', 'col'), as said below
- rotations: float32 [2, 16, 768, 768], P(None, 'row', 'col')
- flips: int32 [2, 16], replicated, may hold values from 0 to 1
Outputs:
- result: float32 [12288, 12288], P('row', 'col')
Inputs may be any that keep to these rules, and one draw needn't show every extreme that they name: `matrix`: symmetric.
All inputs are finite; a program needn't handle non-finite values.
Results may differ from a plain program's by a relative error of at most 0.00013.
Values sent between devices are 32-bit elements; how exact they have to be, the bound alone decides.
No kernel may reach another device: no remote copies, remote signals or barrier semaphores. Data moves between devices by JAX's collectives and lax.ppermute only.
A program may use at most 64 MiB of HBM per device.

v0:
```python
import jax
import jax.numpy as jnp
from jax import lax
from jax.sharding import PartitionSpec as P


def spread(value, axis, root):
    mine = lax.axis_index(axis) == root
    return lax.psum(jnp.where(mine, value, jnp.zeros_like(value)), axis)


def shifted(value, axis, steps):
    count = lax.axis_size(axis)
    initial, last = (max(0, -steps), min(count, count - steps))
    return lax.ppermute(value, axis, [(source, source + steps) for source in range(initial, last)])


def prepare(blocks, flip, pdim, start):
    tops = lax.index_in_dim(blocks, 0, pdim + 1, keepdims=False)
    bots = lax.index_in_dim(blocks, 1, pdim + 1, keepdims=False)
    tops, bots = (jnp.where(flip, bots, tops), jnp.where(flip, tops, bots))
    local = tops.shape[pdim]
    shape = [1] * tops.ndim
    shape[pdim] = local
    place = (start + jnp.arange(local, dtype=jnp.int32)).reshape(shape)
    sendup = jnp.where(place == 0, bots, tops)
    return (tops, bots, sendup, place, sendup, bots)


def assemble(tops, bots, sendup, place, incoming_up, incoming_down, pdim, total):
    local = tops.shape[pdim]
    new_top = jnp.concatenate(
        [incoming_up, lax.slice_in_dim(sendup, 0, local - 1, axis=pdim)], axis=pdim
    )
    new_top = jnp.where(place == 0, tops, new_top)
    new_bot = jnp.concatenate(
        [lax.slice_in_dim(bots, 1, local, axis=pdim), incoming_down], axis=pdim
    )
    new_bot = jnp.where(place == total - 1, tops, new_bot)
    return jnp.stack([new_top, new_bot], axis=pdim + 1)


def on_device(matrix, rotations, flips):
    rows_local, cols_local = matrix.shape
    block = rows_local // 2
    n_row = lax.axis_size("row")
    n_col = lax.axis_size("col")
    per_col = n_row // n_col
    row_id = lax.axis_index("row")
    col_id = lax.axis_index("col")
    steps = rotations.shape[0]
    current = matrix
    for step in range(steps):
        piece = rotations[step, 0]
        row_rot = lax.all_gather(piece, "col", axis=0, tiled=True)
        root = col_id * per_col + 0
        factors = [spread(row_rot, "row", root)]
        col_rots = jnp.stack(factors, axis=0)
        left = lax.dot_general(
            row_rot,
            current,
            (((0,), (0,)), ((), ())),
            precision=lax.Precision.HIGHEST,
            preferred_element_type=jnp.float32,
        )
        both = jnp.einsum(
            "ikb,kbc->ikc",
            left.reshape(rows_local, per_col, rows_local),
            col_rots,
            precision=lax.Precision.HIGHEST,
            preferred_element_type=jnp.float32,
        )
        current = both.reshape(rows_local, cols_local)
        marks = flips[step] == 1
        row_flip = lax.dynamic_slice_in_dim(marks, row_id, 1).reshape(1, 1, 1)
        blocks = current.reshape(1, 2, block, cols_local)
        tops, bots, sendup, place, last_up, first_bot = prepare(blocks, row_flip, 0, row_id)
        incoming_up = shifted(last_up, "row", 1)
        incoming_down = shifted(first_bot, "row", -1)
        current = assemble(tops, bots, sendup, place, incoming_up, incoming_down, 0, n_row).reshape(
            rows_local, cols_local
        )
        col_flip = lax.dynamic_slice_in_dim(marks, col_id * per_col, per_col).reshape(1, per_col, 1)
        blocks = current.reshape(rows_local, per_col, 2, block)
        tops, bots, sendup, place, last_up, first_bot = prepare(
            blocks, col_flip, 1, col_id * per_col
        )
        incoming_up = shifted(last_up, "col", 1)
        incoming_down = shifted(first_bot, "col", -1)
        current = assemble(tops, bots, sendup, place, incoming_up, incoming_down, 1, n_row).reshape(
            rows_local, cols_local
        )
    return current


def solution(mesh):
    in_specs = (P("row", "col"), P(None, "row", "col", None), P())
    out_specs = P("row", "col")
    return jax.shard_map(
        on_device, mesh=mesh, in_specs=in_specs, out_specs=out_specs, check_vma=False
    )
```

profile of v0, /device:TPU:121, one launch (start us, length us, event | category | flops | bytes accessed | tf_op | source)
XLA Modules:
  0.0 574.4 jit_solution(6579898771510567194)
XLA Ops:
  9.2 38.7 %all-gather.5.cloned.1.call-done = f32[1,1,768,768]{3,2,1,0:T(8,128)} async-done(((f32[1,1,48,768]{3,2,1,0:T(8,128)}), f32[1,1,768,768]{3,2,1,0:T(8,128)}) %all-gather.5.cloned.1.call-update) | async-done | bytes 2359312 | tf_op jit(solution)/shard_map/all_gather | solution.py:55
  47.9 3.2 bitcast_select_fusion.1
  51.1 35.5 %all-gather.7.cloned.1.call-done = f32[1,1,768,768]{3,2,1,0:T(8,128)} async-done(((f32[1,1,48,768]{3,2,1,0:T(8,128)}), f32[1,1,768,768]{3,2,1,0:T(8,128)}) %all-gather.7.cloned.1.call-update) | async-done | bytes 2359312 | tf_op jit(solution)/shard_map/all_gather | solution.py:55
  86.6 3.2 bitcast_select_fusion
  91.2 8.5 %fusion = f32[768,768]{1,0:T(8,128)} fusion(f32[768,768]{1,0:T(8,128)S(1)} %copy-done, f32[1,1,768,768]{3,2,1,0:T(8,128)} %all-gather.7.cloned.1.call-done), kind=kOutput, calls=%fused_computation.4 | convolution fusion | flops 5435817984 | bytes 7077888 | tf_op jit(solution)/shard_map/dot_general | solution.py:59
  99.7 219.2 %all-reduce.3.cloned.1.call-done = (f32[768,768]{1,0:T(8,128)}, f32[768,768]{1,0:T(8,128)}) async-done(((f32[768,768]{1,0:T(8,128)}, f32[768,768]{1,0:T(8,128)}), (f32[768,768]{1,0:T(8,128)}, f32[768,768]{1,0:T(8,128)})) %all-reduce.3.cloned.1.call-update) | async-done | bytes 4718608 | tf_op jit(solution)/shard_map/psum | solution.py:9
  318.9 8.2 %fusion.21 = f32[768,768]{0,1:T(8,128)S(1)} fusion(f32[768,768]{1,0:T(8,128)} %get-tuple-element.6, f32[768,768]{1,0:T(8,128)} %fusion), kind=kOutput, calls=%fused_computation.49 | convolution fusion | flops 5435817984 | bytes 7077888 | tf_op jit(solution)/shard_map/ikb,kbc->ikc/dot_general | solution.py:66
  329.4 3.6 collective-permute-start
  335.8 47.9 %collective-permute-done = f32[1,384,768]{2,1,0:T(8,128)S(1)} collective-permute-done((f32[1,384,768]{2,1,0:T(8,128)}, f32[1,384,768]{2,1,0:T(8,128)S(1)}, u32[]{:S(2)}, u32[]{:S(2)}) %collective-permute-start) | collective-permute-done | bytes 1179680 | tf_op jit(solution)/shard_map/ppermute | solution.py:15
  389.2 3.7 reshape_reshape.16
  392.9 3.8 broadcast_select_fusion.9
  396.6 11.3 %collective-permute-start.2 = (f32[768,1,384]{2,1,0:T(1,128)}, f32[768,1,384]{2,1,0:T(1,128)S(1)}, u32[]{:S(2)}, u32[]{:S(2)}) collective-permute-start(f32[768,1,384]{2,1,0:T(1,128)} %get-tuple-element.13), channel_id=1, source_target_pairs={{0,1},{1,2},{2,3},{3,4},{4,5},{5,6},{6,7},{7,8},{8,9},{9,10},{10,1... | collective-permute-start | bytes 3538952 | tf_op jit(solution)/shard_map/ppermute | solution.py:15
  410.5 23.5 %collective-permute-done.2 = f32[768,1,384]{2,1,0:T(1,128)S(1)} collective-permute-done((f32[768,1,384]{2,1,0:T(1,128)}, f32[768,1,384]{2,1,0:T(1,128)S(1)}, u32[]{:S(2)}, u32[]{:S(2)}) %collective-permute-start.2) | collective-permute-done | bytes 1179680 | tf_op jit(solution)/shard_map/ppermute | solution.py:15
  436.1 3.6 fusion.4
  439.8 7.7 %maximum_reduce_fusion = f32[768,2,384]{2,1,0:T(2,128)S(1)} fusion(f32[768,1,1,384]{3,1,2,0:T(1,128)S(1)} %get-tuple-element.24, f32[768,1,1,384]{3,1,2,0:T(1,128)S(1)} %get-tuple-element.23), kind=kLoop, calls=%fused_computation.1 | loop fusion | flops 589824 | bytes 4718592 | tf_op jit(solution)/shard_map/stack | solution.py:40
  449.1 6.8 %fusion.2 = f32[768,768]{1,0:T(8,128)S(1)} fusion(f32[768,768]{1,0:T(8,128)S(1)} %bitcast.92, f32[1,1,768,768]{3,2,1,0:T(8,128)S(1)} %copy-done.2), kind=kOutput, calls=%fused_computation.7 | convolution fusion | flops 5435817984 | bytes 7077888 | tf_op jit(solution)/shard_map/dot_general | solution.py:59
  456.0 6.3 %fusion.22 = f32[768,768]{0,1:T(8,128)S(1)} fusion(f32[768,768]{1,0:T(8,128)S(1)} %copy-done.3, f32[768,768]{1,0:T(8,128)S(1)} %fusion.2), kind=kOutput, calls=%fused_computation.50 | convolution fusion | flops 5435817984 | bytes 7077888 | tf_op jit(solution)/shard_map/ikb,kbc->ikc/dot_general | solution.py:66
  463.3 3.8 collective-permute-start.4
  469.7 36.8 %collective-permute-done.4 = f32[1,384,768]{2,1,0:T(8,128)S(1)} collective-permute-done((f32[1,384,768]{2,1,0:T(8,128)S(1)}, f32[1,384,768]{2,1,0:T(8,128)S(1)}, u32[]{:S(2)}, u32[]{:S(2)}) %collective-permute-start.4) | collective-permute-done | bytes 1179680 | tf_op jit(solution)/shard_map/ppermute | solution.py:15
  506.5 3.4 collective-permute-done.5
  511.6 3.7 reshape_reshape.17
  518.0 14.9 %collective-permute-start.6 = (f32[768,1,384]{2,1,0:T(1,128)S(1)}, f32[768,1,384]{2,1,0:T(1,128)S(1)}, u32[]{:S(2)}, u32[]{:S(2)}) collective-permute-start(f32[768,1,384]{2,1,0:T(1,128)S(1)} %get-tuple-element.7), channel_id=1, source_target_pairs={{0,1},{1,2},{2,3},{3,4},{4,5},{5,6},{6,7},{7,8},{8,9},{9,10},{10,1... | collective-permute-start | bytes 3538952 | tf_op jit(solution)/shard_map/ppermute | solution.py:15
  534.9 14.1 %collective-permute-done.6 = f32[768,1,384]{2,1,0:T(1,128)S(1)} collective-permute-done((f32[768,1,384]{2,1,0:T(1,128)S(1)}, f32[768,1,384]{2,1,0:T(1,128)S(1)}, u32[]{:S(2)}, u32[]{:S(2)}) %collective-permute-start.6) | collective-permute-done | bytes 1179680 | tf_op jit(solution)/shard_map/ppermute | solution.py:15
  549.0 11.8 %collective-permute-done.7 = f32[768,1,384]{2,1,0:T(1,128)S(1)} collective-permute-done((f32[768,1,384]{2,1,0:T(1,128)S(1)}, f32[768,1,384]{2,1,0:T(1,128)S(1)}, u32[]{:S(2)}, u32[]{:S(2)}) %collective-permute-start.7) | collective-permute-done | bytes 1179680 | tf_op jit(solution)/shard_map/ppermute | solution.py:15
  (45 shorter events, 37.5 us)
Async XLA Ops:
  6.5 84.7 %copy-start = (f32[768,768]{1,0:T(8,128)S(1)}, f32[768,768]{1,0:T(8,128)}, u32[]{:S(2)}) copy-start(f32[768,768]{1,0:T(8,128)} %param.3) | copy-start | bytes 7077892
  6.5 41.4 %all-gather.5.cloned.1.call-start = ((), (), s32[]{:S(2)}) async-start(), calls=%async_computation | async-start | bytes 2506752 | tf_op jit(solution)/shard_map/all_gather | solution.py:55
  8.4 78.2 %all-gather.7.cloned.1.call-start = ((), (), s32[]{:S(2)}) async-start(), calls=%async_computation.1 | async-start | bytes 2506752 | tf_op jit(solution)/shard_map/all_gather | solution.py:55
  9.2 309.7 %all-reduce.3.cloned.1.call-start = ((), (), s32[]{:S(2)}) async-start(), calls=%async_computation.2 | async-start | bytes 9437184 | tf_op jit(solution)/shard_map/psum | solution.py:9
  89.8 0.7 copy-start.8
  329.4 54.3 %collective-permute-start = (f32[1,384,768]{2,1,0:T(8,128)}, f32[1,384,768]{2,1,0:T(8,128)S(1)}, u32[]{:S(2)}, u32[]{:S(2)}) collective-permute-start(f32[1,384,768]{2,1,0:T(8,128)} %get-tuple-element.16), channel_id=1, source_target_pairs={{0,16},{16,32},{32,48},{48,64},{64,80},{80,96},{96,112},{112,128},... | collective-permute-start | bytes 3538952 | tf_op jit(solution)/shard_map/ppermute | solution.py:15
  333.0 50.6 %collective-permute-start.1 = (f32[1,384,768]{2,1,0:T(8,128)}, f32[1,384,768]{2,1,0:T(8,128)S(1)}, u32[]{:S(2)}, u32[]{:S(2)}) collective-permute-start(f32[1,384,768]{2,1,0:T(8,128)} %get-tuple-element.18), channel_id=1, source_target_pairs={{16,0},{32,16},{48,32},{64,48},{80,64},{96,80},{112,96},{128,112},... | collective-permute-start | bytes 3538952 | tf_op jit(solution)/shard_map/ppermute | solution.py:15
  383.7 1.0 copy-start.6
  384.7 1.0 copy-start.7
  396.6 37.4 %collective-permute-start.2 = (f32[768,1,384]{2,1,0:T(1,128)}, f32[768,1,384]{2,1,0:T(1,128)S(1)}, u32[]{:S(2)}, u32[]{:S(2)}) collective-permute-start(f32[768,1,384]{2,1,0:T(1,128)} %get-tuple-element.13), channel_id=1, source_target_pairs={{0,1},{1,2},{2,3},{3,4},{4,5},{5,6},{6,7},{7,8},{8,9},{9,10},{10,1... | collective-permute-start | bytes 3538952 | tf_op jit(solution)/shard_map/ppermute | solution.py:15
  407.9 27.2 %collective-permute-start.3 = (f32[768,1,384]{2,1,0:T(1,128)}, f32[768,1,384]{2,1,0:T(1,128)S(1)}, u32[]{:S(2)}, u32[]{:S(2)}) collective-permute-start(f32[768,1,384]{2,1,0:T(1,128)} %get-tuple-element.14), channel_id=1, source_target_pairs={{1,0},{2,1},{3,2},{4,3},{5,4},{6,5},{7,6},{8,7},{9,8},{10,9},{11,1... | collective-permute-start | bytes 3538952 | tf_op jit(solution)/shard_map/ppermute | solution.py:15
  434.0 1.1 copy-start.4
  435.1 1.1 copy-start.5
  447.5 1.7 copy-start.2
  449.1 6.8 %copy-start.3 = (f32[768,768]{1,0:T(8,128)S(1)}, f32[768,768]{1,0:T(8,128)}, u32[]{:S(2)}) copy-start(f32[768,768]{1,0:T(8,128)} %get-tuple-element.5) | copy-start | bytes 7077892
  463.3 43.2 %collective-permute-start.4 = (f32[1,384,768]{2,1,0:T(8,128)S(1)}, f32[1,384,768]{2,1,0:T(8,128)S(1)}, u32[]{:S(2)}, u32[]{:S(2)}) collective-permute-start(f32[1,384,768]{2,1,0:T(8,128)S(1)} %get-tuple-element.10), channel_id=1, source_target_pairs={{0,16},{16,32},{32,48},{48,64},{64,80},{80,96},{96,112},{112,128},... | collective-permute-start | bytes 3538952 | tf_op jit(solution)/shard_map/ppermute | solution.py:15
  467.1 42.7 %collective-permute-start.5 = (f32[1,384,768]{2,1,0:T(8,128)S(1)}, f32[1,384,768]{2,1,0:T(8,128)S(1)}, u32[]{:S(2)}, u32[]{:S(2)}) collective-permute-start(f32[1,384,768]{2,1,0:T(8,128)S(1)} %get-tuple-element.12), channel_id=1, source_target_pairs={{16,0},{32,16},{48,32},{64,48},{80,64},{96,80},{112,96},{128,112},... | collective-permute-start | bytes 3538952 | tf_op jit(solution)/shard_map/ppermute | solution.py:15
  518.0 30.9 %collective-permute-start.6 = (f32[768,1,384]{2,1,0:T(1,128)S(1)}, f32[768,1,384]{2,1,0:T(1,128)S(1)}, u32[]{:S(2)}, u32[]{:S(2)}) collective-permute-start(f32[768,1,384]{2,1,0:T(1,128)S(1)} %get-tuple-element.7), channel_id=1, source_target_pairs={{0,1},{1,2},{2,3},{3,4},{4,5},{5,6},{6,7},{7,8},{8,9},{9,10},{10,1... | collective-permute-start | bytes 3538952 | tf_op jit(solution)/shard_map/ppermute | solution.py:15
  533.0 27.8 %collective-permute-start.7 = (f32[768,1,384]{2,1,0:T(1,128)S(1)}, f32[768,1,384]{2,1,0:T(1,128)S(1)}, u32[]{:S(2)}, u32[]{:S(2)}) collective-permute-start(f32[768,1,384]{2,1,0:T(1,128)S(1)} %get-tuple-element.8), channel_id=1, source_target_pairs={{1,0},{2,1},{3,2},{4,3},{5,4},{6,5},{7,6},{8,7},{9,8},{10,9},{11,1... | collective-permute-start | bytes 3538952 | tf_op jit(solution)/shard_map/ppermute | solution.py:15
  564.9 2.5 copy-start.1
Sparse Core Ops, SparseCore 0:
  9.2 38.6 all-gather.4
  49.7 36.8 all-gather.6
  90.0 228.8 all-reduce.2
where the time goes:
time: 582 us; the launch traced here: 574 us
  waiting for transfers between devices  433 us (74%)
  starting transfers between devices  42.9 us (7%)
  other arithmetic  36.8 us (6%)
  matrix products  29.8 us (5%)
  local copies, waits for them, and re-layouts  18.5 us (3%)
  between operations  13.8 us (2%)
    psum x1, waiting for transfers between devices, spread(): return lax.psum(jnp.where(mine, value, jnp.zeros_like(value)), axis)  219 us
    ppermute x8, waiting for transfers between devices, shifted(): lax.ppermute(value, axis, [(source, source + steps) for source in range(i...  138 us
    all_gather x2, waiting for transfers between devices, on_device(): row_rot = lax.all_gather(piece, 'col', axis=0, tiled=True)  74.2 us
    ppermute x8, starting transfers between devices, shifted(): lax.ppermute(value, axis, [(source, source + steps) for source in range(i...  42.8 us
    another operation x8, other arithmetic, assemble(): return jnp.stack([new_top, new_bot], axis=pdim + 1)  20.7 us
    dot_general x2, matrix products, on_device(): lax.dot_general(row_rot, current, (((0,), (0,)), ((), ())), precision=lax...  15.3 us
    dot_general x2, matrix products, on_device(): jnp.einsum('ikb,kbc->ikc', left.reshape(rows_local, per_col, rows_local),...  14.5 us
  transfers between devices with their start and end apart: 11, of which 10 were waited for; matrix products, arithmetic and copies ran while one was open for 2% of the time, Pallas kernels for 0%

commit v1 on v0

v1 whole, which is shorter than its diff:
```python
import functools

import jax
import jax.numpy as jnp
import numpy as np
from jax import lax
from jax.experimental import pallas as pl
from jax.experimental.pallas import tpu as pltpu
from jax.sharding import PartitionSpec as P

AXES = ("row", "col")
KERNELS = True
BF = jnp.bfloat16
F32 = jnp.float32
MIRRORED = (
    0x001A2010015A8412,
    0x92451A411A401A6D,
    0x540354011481D4A1,
    0x198A854AAD8A054C,
    0x4450865A8076A858,
    0x1A4912041A451045,
    0x44211481542194A1,
    0x20CAAC8A2548A580,
    0x084B8056A9498812,
    0x52491A4510451A08,
    0x8081D4A190A1D421,
    0xA5886548A5888504,
    0x0CD2885AA058AC52,
    0x1A4510451841108D,
    0x54B1942504A194A1,
    0x2108A120210A2100,
)
PERMUTATION = (
    0x9C36C97893721B8D878DE1D24B2DB139,
    0xB18D4B398778786C2D39396C1E6CD2E4,
    0x3693D278C6B14E72E42D1E93871BE163,
    0x4BB43927D21E1E2DC9728D2D4E366336,
    0x1ED887E4E44E2D781B72B193931E2772,
    0x396C2DE1782D4E93931B36E44E6CD89C,
    0x634E2D391EB17836279C721BE46CD8C6,
    0xC963D8E19C4B4BC963E4D827C9784B63,
    0x6CB14B6C4B4B72D836636C8D4B3963C9,
    0xC69C1E1E637272272DD2E42D4B3987D8,
    0xB18D1E728DC6E11EC972D2274E27B478,
    0xE163784B63C9D28DD84BC6E42DC94E87,
    0x8D36D2D2391B9CE11E87B19C8DC6D2C6,
    0x36B4B4781B87D89C4ED2D21B87392D1E,
    0x72393678E4E11B1E399CC6722D1E2D39,
    0x9C7887C9D24E9CB1399C1B9C39394BE1,
)


def permute(value, where):
    pairs = []
    for row in range(16):
        for col in range(16):
            y, zh, x, zl, c = where(row // 4, row % 4, col // 4, col // 2 % 2, col % 2)
            target = (4 * (y % 4) + zh % 4) * 16 + 4 * (x % 4) + 2 * (zl % 2) + c % 2
            pairs.append((16 * row + col, target))
    return lax.ppermute(value, AXES, pairs)


def after(value, *others):
    return lax.optimization_barrier((value, *others))[0]


def turn_pieces(piece):
    return permute(piece, lambda y, zh, x, zl, c: (x, 2 * zl + c, y, zh >> 1, zh & 1))


def spread_z(turned):
    return [turned] + [
        permute(turned, lambda y, zh, x, zl, c, k=k: (y, zh ^ k, x, zl, c)) for k in (1, 2, 3)
    ]


def spread_y(mine):
    return [mine] + [
        permute(mine, lambda y, zh, x, zl, c, d=d: (y - d, zh, x, zl, c)) for d in (1, 2, 3)
    ]


def swap(kind, i):
    if kind == 0:
        return i ^ 1
    return i if i in (0, 15) else (i + 1 if i % 2 else i - 1)


@functools.cache
def quadrant_moves():
    edges = [[] for _ in range(256)]
    for p in range(16):
        for q in range(16):
            for a in range(2):
                for b in range(2):
                    source, sent = (swap(a, p), swap(b, q)), 2 * a + b
                    flag = MIRRORED[p] >> (4 * q + sent) & 1
                    if flag:
                        source, sent = source[::-1], 2 * b + a
                    edges[16 * p + q].append((16 * source[0] + source[1], sent, 2 * a + b, flag))
    pairs, table = [[] for _ in range(4)], np.zeros((256, 12), np.int32)
    for device in range(256):
        p, q = divmod(device, 16)
        for source, sent, slot, flag in edges[device]:
            m = PERMUTATION[p] >> (8 * q + 2 * slot) & 3
            pairs[m].append((source, device))
            table[source, m] = sent
            table[device, 4 + m] = slot
            table[device, 8 + m] = flag
    for each in pairs:
        assert len({s for s, _ in each}) == len({d for _, d in each}) == len(each) == 256
    return pairs, table


def move(quads):
    quads = lax.optimization_barrier(quads)
    return [lax.ppermute(q, AXES, pairs) for q, pairs in zip(quads, quadrant_moves()[0])]


def split(value):
    high = value.astype(BF)
    return high, (value - high.astype(F32)).astype(BF)


def product(ah, al, bh, bl):
    dot = functools.partial(jnp.dot, preferred_element_type=F32)
    return dot(ah, bh) + (dot(ah, bl) + dot(al, bh))


def col_slots(y, zh, shift):
    return [(4 * ((y + dy) % 4) + (zh ^ k) + shift) % 16 for dy in range(4) for k in range(4)]


def call(kernel, outs, args, flops, scratch=()):
    specs = [pl.BlockSpec(memory_space=pltpu.SMEM)]
    specs += [pl.BlockSpec(memory_space=pltpu.VMEM)] * (len(args) - 1)
    nbytes = sum(a.size * a.dtype.itemsize for a in args) + sum(o.size * o.dtype.itemsize for o in outs)
    return pl.pallas_call(
        kernel,
        out_shape=outs,
        in_specs=specs,
        out_specs=[pl.BlockSpec(memory_space=pltpu.VMEM)] * len(outs),
        scratch_shapes=list(scratch),
        compiler_params=pltpu.CompilerParams(vmem_limit_bytes=32 * 2**20),
        cost_estimate=pl.CostEstimate(flops=flops, bytes_accessed=nbytes, transcendentals=0),
    )(*args)


def shape(dims, dtype):
    return jax.ShapeDtypeStruct(dims, dtype)


def turn_factor(shift, factor):
    wide = factor.shape[1]
    half = wide // 2
    if not KERNELS:
        return split(jnp.roll(factor, shift[0] * half, axis=0).T)

    def kernel(shift_ref, factor_ref, high, low, whole):
        at = pl.multiple_of(shift_ref[0] * half, half)
        whole[pl.ds(at, half), :] = factor_ref[:half, :]
        whole[pl.ds(half - at, half), :] = factor_ref[half:, :]
        high[...], low[...] = split(whole[...].T)

    outs = [shape((wide, wide), BF)] * 2
    return call(kernel, outs, [shift, factor], 0, [pltpu.VMEM((wide, wide), F32)])


def fill_factor(slots_ref, at, refs, piece, high, low):
    count = refs[0].shape[0] // piece
    for n, ref in enumerate(refs):
        for k in range(count):
            to = pl.ds(pl.multiple_of(slots_ref[at + n * count + k] * piece, 16), piece)
            high[to, :], low[to, :] = split(ref[k * piece : (k + 1) * piece, :])


def plain_factor(slots, parts, piece):
    flat = jnp.concatenate(parts, axis=0)
    count = flat.shape[0] // piece
    flat = flat.reshape(count, piece, flat.shape[1])
    order = jnp.zeros((count,), jnp.int32).at[slots].set(jnp.arange(count, dtype=jnp.int32))
    return split(jnp.take(flat, order, axis=0).reshape(count * piece, -1))


def column_factor(slots, parts, piece):
    wide = parts[0].shape[1]
    if not KERNELS:
        return plain_factor(slots, parts, piece)

    def kernel(slots_ref, *refs):
        ins, (high, low) = refs[: len(parts)], refs[len(parts) :]
        fill_factor(slots_ref, 0, ins, piece, high, low)

    return call(kernel, [shape((wide, wide), BF)] * 2, [slots, *parts], 0)


def left(turned, block):
    wide = block.shape[0]
    if not KERNELS:
        return split(product(*turned, *split(block)))

    def kernel(_, ah, al, ref, high, low, xh, xl):
        xh[...], xl[...] = split(ref[...])

        @pl.loop(0, wide // 256)
        def _(i):
            here = pl.ds(pl.multiple_of(i * 256, 256), 256)
            high[here, :], low[here, :] = split(product(ah[here, :], al[here, :], xh[...], xl[...]))

    outs = [shape((wide, wide), BF)] * 2
    scratch = [pltpu.VMEM((wide, wide), BF)] * 2
    dummy = jnp.zeros((1,), jnp.int32)
    return call(kernel, outs, [dummy, *turned, block], 6 * wide**3, scratch)


def write_quads(info_ref, th, tl, bh, bl, outs):
    half = bh.shape[0] // 2
    for m, out in enumerate(outs):
        sent = info_ref[m]
        rows = pl.ds(pl.multiple_of(((sent >> 1) ^ info_ref[12]) * half, half), half)
        cols = pl.ds(pl.multiple_of(((sent & 1) ^ info_ref[13]) * half, half), half)
        out[...] = product(th[rows, :], tl[rows, :], bh[:, cols], bl[:, cols])


def plain_quads(info, whole):
    half = whole.shape[0] // 2
    quads = whole.reshape(2, half, 2, half).transpose(0, 2, 1, 3).reshape(4, half, half)
    return [jnp.take(quads, info[m] ^ (2 * info[12] + info[13]), axis=0) for m in range(4)]


def right(info, lefts, parts, piece):
    wide = lefts[0].shape[0]
    half = wide // 2
    if not KERNELS:
        return plain_quads(info, product(*lefts, *plain_factor(info[14:], parts, piece)))

    def kernel(info_ref, th, tl, *refs):
        ins, outs, (bh, bl) = refs[: len(parts)], refs[len(parts) : -2], refs[-2:]
        fill_factor(info_ref, 14, ins, piece, bh, bl)
        write_quads(info_ref, th, tl, bh, bl, outs)

    outs = [shape((half, half), F32)] * 4
    scratch = [pltpu.VMEM((wide, wide), BF)] * 2
    return call(kernel, outs, [info, *lefts, *parts], 6 * wide**3, scratch)


def place_quads(table_ref, refs, store, swap_rows=0, swap_cols=0):
    half = refs[0].shape[0]
    for m, ref in enumerate(refs):
        slot = table_ref[4 + m]
        rows = pl.ds(pl.multiple_of(((slot >> 1) ^ swap_rows) * half, half), half)
        cols = pl.ds(pl.multiple_of(((slot & 1) ^ swap_cols) * half, half), half)

        @pl.when(table_ref[8 + m] == 0)
        def _():
            store(rows, cols, ref[...])

        @pl.when(table_ref[8 + m] != 0)
        def _():
            store(rows, cols, ref[...].T)


def plain_block(table, quads, swap_rows=0, swap_cols=0):
    half = quads[0].shape[0]
    whole = jnp.zeros((2 * half, 2 * half), F32)
    for m, quad in enumerate(quads):
        slot = table[4 + m]
        at = (((slot >> 1) ^ swap_rows) * half, ((slot & 1) ^ swap_cols) * half)
        whole = lax.dynamic_update_slice(whole, jnp.where(table[8 + m] == 0, quad, quad.T), at)
    return whole


def both_sides(info, turned, factor, quads):
    half = quads[0].shape[0]
    wide = 2 * half
    if not KERNELS:
        middle = split(product(*turned, *split(plain_block(info, quads))))
        return plain_quads(info, product(*middle, *factor))

    def kernel(info_ref, ah, al, bh, bl, *refs):
        ins, outs, (xh, xl, th, tl) = refs[:4], refs[4:8], refs[8:]

        def store(rows, cols, value):
            xh[rows, cols], xl[rows, cols] = split(value)

        place_quads(info_ref, ins, store)

        @pl.loop(0, wide // 256)
        def _(i):
            here = pl.ds(pl.multiple_of(i * 256, 256), 256)
            th[here, :], tl[here, :] = split(product(ah[here, :], al[here, :], xh[...], xl[...]))

        write_quads(info_ref, th, tl, bh, bl, outs)

    outs = [shape((half, half), F32)] * 4
    scratch = [pltpu.VMEM((wide, wide), BF)] * 4
    return call(kernel, outs, [info, *turned, *factor, *quads], 12 * wide**3, scratch)


def whole_block(table, quads, odd_rows, odd_cols):
    half = quads[0].shape[0]
    if not KERNELS:
        return plain_block(table, quads, 1 - odd_rows, 1 - odd_cols)

    def kernel(info_ref, *refs):
        ins, out = refs[:4], refs[4]

        def store(rows, cols, value):
            out[rows, cols] = value

        place_quads(info_ref, ins, store, 1 - info_ref[12], 1 - info_ref[13])

    info = jnp.concatenate([table, jnp.stack([odd_rows, odd_cols])])
    return call(kernel, [shape((2 * half, 2 * half), F32)], [info, *quads], 0)[0]


def on_device(matrix, rotations, flips):
    wide = matrix.shape[0]
    half = wide // 2
    piece = rotations.shape[2]
    f = lax.axis_index("row")
    g = lax.axis_index("col")
    y, zh = f // 4, f % 4
    odd_f, odd_g = f % 2, g % 2
    far_first = jnp.where((odd_f == 1) | (f == 0), 1, 0)
    table = lax.dynamic_index_in_dim(jnp.asarray(quadrant_moves()[1]), 16 * f + g, keepdims=False)

    def vector(values):
        return jnp.stack([jnp.asarray(v, jnp.int32) for v in values])

    def halves(step):
        marks = flips[step]
        here = [lax.dynamic_index_in_dim(marks, i, keepdims=False) for i in (f, g)]
        return [here[0] ^ far_first, here[1] ^ jnp.where((odd_g == 1) | (g == 0), 1, 0)]

    rows = [lax.all_gather(rotations[s, 0], "col", axis=0, tiled=True) for s in range(2)]
    four = spread_z(turn_pieces(rotations.reshape(2 * piece, wide)))
    col1 = spread_y(jnp.concatenate([v[:piece] for v in four], axis=0))
    mine2 = jnp.concatenate([v[piece:] for v in four], axis=0)
    middle = left(turn_factor(vector([0]), rows[0]), matrix)
    col2 = spread_y(after(mine2, *col1[1:], middle[0]))
    info1 = jnp.concatenate([table, vector(halves(0) + col_slots(y, zh, 0))])
    moved = move(right(info1, middle, col1, piece))
    turned = turn_factor(vector([1 - odd_f]), after(rows[1], moved[0]))
    slots = vector(col_slots(y, zh, 8 - 8 * odd_g))
    factor = column_factor(slots, col2, piece)
    info2 = jnp.concatenate([table, vector(halves(1))])
    moved = move(both_sides(info2, turned, factor, moved))
    return whole_block(table, moved, odd_f, odd_g)


def solution(mesh):
    in_specs = (P("row", "col"), P(None, "row", "col", None), P())
    out_specs = P("row", "col")
    return jax.shard_map(
        on_device, mesh=mesh, in_specs=in_specs, out_specs=out_specs, check_vma=False
    )
```

time: 582 us -> 245 us (0.42); the launches traced: 574 us -> 244 us
  waiting for transfers between devices: 433 us -> 142 us
  other arithmetic: 36.8 us -> 0.16 us
  matrix products: 29.8 us -> 0 us
  Pallas kernels: 0 us -> 23.1 us
  starting transfers between devices: 42.9 us -> 55.3 us
  local copies, waits for them, and re-layouts: 18.5 us -> 7.5 us
    psum x1 -> x0, waiting for transfers between devices: 219 us -> none  [spread(): return lax.psum(jnp.where(mine, value, jnp.zeros_like(value)), axis)]
    all_gather x2, waiting for transfers between devices: 74.2 us -> 0.02 us  [on_device(): lax.all_gather(rotations[s, 0], 'col', axis=0, tiled=True)]
    dot_general x4 -> x0, matrix products: 29.8 us -> none  [the longest x2 15.3 us: on_device(): lax.dot_general(row_rot, current, (((0,), (0,)), ((), ())), precision=lax...]
    pallas_call x0 -> x7, Pallas kernels: none -> 23.1 us  [call(): pl.pallas_call(kernel, out_shape=outs, in_specs=specs, out_specs=[pl.Bloc...]
    another operation x8 -> x0, other arithmetic: 20.7 us -> none  [assemble(): return jnp.stack([new_top, new_bot], axis=pdim + 1)]
    select_n x6 -> x0, other arithmetic: 16.2 us -> none  [the longest x4 9.75 us: prepare(): sendup = jnp.where(place == 0, bots, tops)]
    ppermute x8 -> x18, starting transfers between devices: 42.8 us -> 55.2 us  [the longest x8 33.4 us: move(): lax.ppermute(q, AXES, pairs)]
    another operation x2 -> x1, local copies, waits for them, and re-layouts: 7.39 us -> 0.09 us  [vector(): return jnp.stack([jnp.asarray(v, jnp.int32) for v in values])]
  transfers between devices with their start and end apart: 11 -> 20, of which waited for: 10 -> 13; matrix products, arithmetic and copies ran while one was open for 2% -> 1% of each run, Pallas kernels for 0% -> 5%
where the time goes in v1:
time: 245 us; the launch traced here: 244 us
  waiting for transfers between devices  142 us (58%)
  starting transfers between devices  55.3 us (23%)
  Pallas kernels  23.1 us (9%)
  between operations  16.6 us (7%)
  local copies, waits for them, and re-layouts  7.5 us (3%)
    ppermute x8, waiting for transfers between devices, move(): lax.ppermute(q, AXES, pairs)  85 us
    ppermute x10, waiting for transfers between devices, permute(): return lax.ppermute(value, AXES, pairs)  55.9 us
    ppermute x8, starting transfers between devices, move(): lax.ppermute(q, AXES, pairs)  33.4 us
    pallas_call x7, Pallas kernels, call(): pl.pallas_call(kernel, out_shape=outs, in_specs=specs, out_specs=[pl.Bloc...  23.1 us
    ppermute x10, starting transfers between devices, permute(): return lax.ppermute(value, AXES, pairs)  21.8 us
  transfers between devices with their start and end apart: 20, of which 13 were waited for; matrix products, arithmetic and copies ran while one was open for 1% of the time, Pallas kernels for 5%

profile of v1, /device:TPU:121, one launch (start us, length us, event | category | flops | bytes accessed | tf_op | source)
XLA Modules:
  0.0 244.2 jit_solution(8965400911862108501)
XLA Ops:
  9.0 7.5 %collective-permute-start = (f32[96,768]{1,0:T(8,128)}, f32[96,768]{1,0:T(8,128)S(1)}, u32[]{:S(2)}, u32[]{:S(2)}) collective-permute-start(f32[96,768]{1,0:T(8,128)} %bitcast.50), channel_id=1, source_target_pairs={{0,0},{1,16},{2,32},{3,48},{4,64},{5,80},{6,96},{7,112},{8,128},{9... | collective-permute-start | bytes 884744 | tf_op jit(solution)/shard_map/ppermute | solution.py:60
  16.5 12.2 %collective-permute-done = f32[96,768]{1,0:T(8,128)S(1)} collective-permute-done((f32[96,768]{1,0:T(8,128)}, f32[96,768]{1,0:T(8,128)S(1)}, u32[]{:S(2)}, u32[]{:S(2)}) %collective-permute-start) | collective-permute-done | bytes 294944 | tf_op jit(solution)/shard_map/ppermute | solution.py:60
  29.1 4.6 %collective-permute-start.2 = (f32[96,768]{1,0:T(8,128)S(1)}, f32[96,768]{1,0:T(8,128)S(1)}, u32[]{:S(2)}, u32[]{:S(2)}) collective-permute-start(f32[96,768]{1,0:T(8,128)S(1)} %collective-permute-done), channel_id=1, source_target_pairs={{0,32},{1,33},{2,34},{3,35},{4,36},{5,37},{6,38},{7,39},{8,40},{9,... | collective-permute-start | bytes 884744 | tf_op jit(solution)/shard_map/ppermute | solution.py:60
  34.4 8.7 %collective-permute-done.1 = f32[96,768]{1,0:T(8,128)S(1)} collective-permute-done((f32[96,768]{1,0:T(8,128)S(1)}, f32[96,768]{1,0:T(8,128)S(1)}, u32[]{:S(2)}, u32[]{:S(2)}) %collective-permute-start.1) | collective-permute-done | bytes 294944 | tf_op jit(solution)/shard_map/ppermute | solution.py:60
  43.1 21.2 %collective-permute-done.2 = f32[96,768]{1,0:T(8,128)S(1)} collective-permute-done((f32[96,768]{1,0:T(8,128)S(1)}, f32[96,768]{1,0:T(8,128)S(1)}, u32[]{:S(2)}, u32[]{:S(2)}) %collective-permute-start.2) | collective-permute-done | bytes 294944 | tf_op jit(solution)/shard_map/ppermute | solution.py:60
  64.5 2.6 %collective-permute-start.4 = (f32[192,768]{1,0:T(8,128)S(1)}, f32[192,768]{1,0:T(8,128)S(1)}, u32[]{:S(2)}, u32[]{:S(2)}) collective-permute-start(f32[192,768]{1,0:T(8,128)S(1)} %pad_maximum_fusion.refs_0_), channel_id=1, source_target_pairs={{0,192},{1,193},{2,194},{3,195},{4,196},{5,197},{6,198},{7,199},{8... | collective-permute-start | bytes 1769480 | tf_op jit(solution)/shard_map/ppermute | solution.py:60
  67.0 2.5 %collective-permute-start.6 = (f32[192,768]{1,0:T(8,128)S(1)}, f32[192,768]{1,0:T(8,128)S(1)}, u32[]{:S(2)}, u32[]{:S(2)}) collective-permute-start(f32[192,768]{1,0:T(8,128)S(1)} %pad_maximum_fusion.refs_0_), channel_id=1, source_target_pairs={{0,64},{1,65},{2,66},{3,67},{4,68},{5,69},{6,70},{7,71},{8,72},{9,... | collective-permute-start | bytes 1769480 | tf_op jit(solution)/shard_map/ppermute | solution.py:60
  75.7 3.7 %shard_map.47 = (bf16[768,768]{1,0:T(8,128)(2,1)S(1)}, bf16[768,768]{1,0:T(8,128)(2,1)S(1)}) custom-call(s32[1]{0:T(128)} %constant.277.clone.1.shift_ref._, bf16[768,768]{1,0:T(8,128)(2,1)S(1)} %get-tuple-element.23.ah, bf16[768,768]{1,0:T(8,128)(2,1)S(1)} %get-tuple-element.24.al, f32[768,768]{1,0:T(8,128)S(1)} %copy-done.2), custom_call_target="tpu_custom_call" | custom-call | flops 2717908992 | bytes 7077892 | tf_op jit(solution)/shard_map/pallas_call | solution.py:138
  80.8 8.6 %collective-permute-done.5.refs_2_ = f32[192,768]{1,0:T(8,128)S(1)} collective-permute-done((f32[192,768]{1,0:T(8,128)S(1)}, f32[192,768]{1,0:T(8,128)S(1)}, u32[]{:S(2)}, u32[]{:S(2)}) %collective-permute-start.5) | collective-permute-done | bytes 589856 | tf_op jit(solution)/shard_map/ppermute | solution.py:60
  89.4 3.7 %collective-permute-done.6.refs_3_ = f32[192,768]{1,0:T(8,128)S(1)} collective-permute-done((f32[192,768]{1,0:T(8,128)S(1)}, f32[192,768]{1,0:T(8,128)S(1)}, u32[]{:S(2)}, u32[]{:S(2)}) %collective-permute-start.6) | collective-permute-done | bytes 589856 | tf_op jit(solution)/shard_map/ppermute | solution.py:60
  93.2 3.4 %collective-permute-start.10 = (f32[192,768]{1,0:T(8,128)S(1)}, f32[192,768]{1,0:T(8,128)S(1)}, u32[]{:S(2)}, u32[]{:S(2)}) collective-permute-start(f32[192,768]{1,0:T(8,128)S(1)} %pad_maximum_fusion.1.refs_0_), channel_id=1, source_target_pairs={{0,64},{1,65},{2,66},{3,67},{4,68},{5,69},{6,70},{7,71},{8,72},{9,... | collective-permute-start | bytes 1769480 | tf_op jit(solution)/shard_map/ppermute | solution.py:60
  96.6 5.5 %shard_map.48 = (f32[384,384]{1,0:T(8,128)S(1)}, f32[384,384]{1,0:T(8,128)}, f32[384,384]{1,0:T(8,128)}, f32[384,384]{1,0:T(8,128)}) custom-call(s32[30]{0:T(128)S(1)} %concatenate.17.info_ref, bf16[768,768]{1,0:T(8,128)(2,1)S(1)} %get-tuple-element.25.th, bf16[768,768]{1,0:T(8,128)(2,1)S(1)} %get-tuple-element.26.tl, ...), custom_call_target="tpu_custom_call" | custom-call | flops 2717908992 | bytes 7078008 | tf_op jit(solution)/shard_map/pallas_call | solution.py:138
  102.1 9.3 %collective-permute-start.7 = (f32[384,384]{1,0:T(8,128)S(1)}, f32[384,384]{1,0:T(8,128)S(1)}, u32[]{:S(2)}, u32[]{:S(2)}) collective-permute-start(f32[384,384]{1,0:T(8,128)S(1)} %get-tuple-element.27), channel_id=1, source_target_pairs={{0,0},{18,1},{1,2},{2,3},{49,4},{22,5},{7,6},{6,7},{9,8},{10,9},{2... | collective-permute-start | bytes 1769480 | tf_op jit(solution)/shard_map/ppermute | solution.py:117
  113.5 5.9 %collective-permute-start.12 = (f32[384,384]{1,0:T(8,128)}, f32[384,384]{1,0:T(8,128)}, u32[]{:S(2)}, u32[]{:S(2)}) collective-permute-start(f32[384,384]{1,0:T(8,128)} %get-tuple-element.35), channel_id=1, source_target_pairs={{1,0},{2,1},{48,2},{20,3},{21,4},{64,5},{5,6},{8,7},{7,8},{26,9},{... | collective-permute-start | bytes 1769480 | tf_op jit(solution)/shard_map/ppermute | solution.py:117
  119.4 19.8 %collective-permute-done.7.refs_0_ = f32[384,384]{1,0:T(8,128)S(1)} collective-permute-done((f32[384,384]{1,0:T(8,128)S(1)}, f32[384,384]{1,0:T(8,128)S(1)}, u32[]{:S(2)}, u32[]{:S(2)}) %collective-permute-start.7) | collective-permute-done | bytes 589856 | tf_op jit(solution)/shard_map/ppermute | solution.py:117
  148.2 7.9 %collective-permute-done.12.refs_2_ = f32[384,384]{1,0:T(8,128)} collective-permute-done((f32[384,384]{1,0:T(8,128)}, f32[384,384]{1,0:T(8,128)}, u32[]{:S(2)}, u32[]{:S(2)}) %collective-permute-start.12) | collective-permute-done | bytes 589856 | tf_op jit(solution)/shard_map/ppermute | solution.py:117
  156.1 6.6 %collective-permute-done.13.refs_3_ = f32[384,384]{1,0:T(8,128)} collective-permute-done((f32[384,384]{1,0:T(8,128)}, f32[384,384]{1,0:T(8,128)}, u32[]{:S(2)}, u32[]{:S(2)}) %collective-permute-start.13) | collective-permute-done | bytes 589856 | tf_op jit(solution)/shard_map/ppermute | solution.py:117
  162.7 9.0 %shard_map.51 = (f32[384,384]{1,0:T(8,128)S(1)}, f32[384,384]{1,0:T(8,128)S(1)}, f32[384,384]{1,0:T(8,128)S(1)}, f32[384,384]{1,0:T(8,128)S(1)}) custom-call(s32[14]{0:T(128)S(1)} %get-tuple-element.55.info_ref, bf16[768,768]{1,0:T(8,128)(2,1)S(1)} %get-tuple-element.29.ah, bf16[768,768]{1,0:T(8,128)(2,1)S(1)} %get-tuple-element.30.al, ...), custom_call_target="tpu_custom_call" | custom-call | flops 5435817984 | bytes 9437240 | tf_op jit(solution)/shard_map/pallas_call | solution.py:138
  171.7 4.1 %collective-permute-start.14 = (f32[384,384]{1,0:T(8,128)S(1)}, f32[384,384]{1,0:T(8,128)S(1)}, u32[]{:S(2)}, u32[]{:S(2)}) collective-permute-start(f32[384,384]{1,0:T(8,128)S(1)} %get-tuple-element.37), channel_id=1, source_target_pairs={{0,0},{18,1},{1,2},{2,3},{49,4},{22,5},{7,6},{6,7},{9,8},{10,9},{2... | collective-permute-start | bytes 1769480 | tf_op jit(solution)/shard_map/ppermute | solution.py:117
  175.8 3.3 %collective-permute-start.15 = (f32[384,384]{1,0:T(8,128)S(1)}, f32[384,384]{1,0:T(8,128)S(1)}, u32[]{:S(2)}, u32[]{:S(2)}) collective-permute-start(f32[384,384]{1,0:T(8,128)S(1)} %get-tuple-element.38), channel_id=1, source_target_pairs={{17,0},{1,1},{19,2},{64,3},{5,4},{65,5},{113,6},{24,7},{25,8},{8,9... | collective-permute-start | bytes 1769480 | tf_op jit(solution)/shard_map/ppermute | solution.py:117
  181.0 5.0 %collective-permute-start.17 = (f32[384,384]{1,0:T(8,128)S(1)}, f32[384,384]{1,0:T(8,128)S(1)}, u32[]{:S(2)}, u32[]{:S(2)}) collective-permute-start(f32[384,384]{1,0:T(8,128)S(1)} %get-tuple-element.40), channel_id=1, source_target_pairs={{1,0},{0,1},{17,2},{18,3},{48,4},{6,5},{21,6},{22,7},{23,8},{129,9... | collective-permute-start | bytes 1769480 | tf_op jit(solution)/shard_map/ppermute | solution.py:117
  186.0 22.4 %collective-permute-done.14.refs_0_ = f32[384,384]{1,0:T(8,128)S(1)} collective-permute-done((f32[384,384]{1,0:T(8,128)S(1)}, f32[384,384]{1,0:T(8,128)S(1)}, u32[]{:S(2)}, u32[]{:S(2)}) %collective-permute-start.14) | collective-permute-done | bytes 589856 | tf_op jit(solution)/shard_map/ppermute | solution.py:117
  208.4 3.2 %collective-permute-done.15.refs_1_ = f32[384,384]{1,0:T(8,128)S(1)} collective-permute-done((f32[384,384]{1,0:T(8,128)S(1)}, f32[384,384]{1,0:T(8,128)S(1)}, u32[]{:S(2)}, u32[]{:S(2)}) %collective-permute-start.15) | collective-permute-done | bytes 589856 | tf_op jit(solution)/shard_map/ppermute | solution.py:117
  211.6 23.4 %collective-permute-done.16.refs_2_ = f32[384,384]{1,0:T(8,128)S(1)} collective-permute-done((f32[384,384]{1,0:T(8,128)S(1)}, f32[384,384]{1,0:T(8,128)S(1)}, u32[]{:S(2)}, u32[]{:S(2)}) %collective-permute-start.16) | collective-permute-done | bytes 589856 | tf_op jit(solution)/shard_map/ppermute | solution.py:117
  (46 shorter events, 23.6 us)
Async XLA Ops:
  6.5 65.8 %all-gather.7.cloned.1.call-start = ((), (), s32[]{:S(2)}) async-start(), calls=%async_computation.1 | async-start | bytes 2506752 | tf_op jit(solution)/shard_map/all_gather | solution.py:336
  8.3 134.9 %all-gather.5.cloned.1.call-start = ((), (), s32[]{:S(2)}) async-start(), calls=%async_computation | async-start | bytes 2506752 | tf_op jit(solution)/shard_map/all_gather | solution.py:336
  9.0 19.7 %collective-permute-start = (f32[96,768]{1,0:T(8,128)}, f32[96,768]{1,0:T(8,128)S(1)}, u32[]{:S(2)}, u32[]{:S(2)}) collective-permute-start(f32[96,768]{1,0:T(8,128)} %bitcast.50), channel_id=1, source_target_pairs={{0,0},{1,16},{2,32},{3,48},{4,64},{5,80},{6,96},{7,112},{8,128},{9... | collective-permute-start | bytes 884744 | tf_op jit(solution)/shard_map/ppermute | solution.py:60
  28.7 14.4 %collective-permute-start.1 = (f32[96,768]{1,0:T(8,128)S(1)}, f32[96,768]{1,0:T(8,128)S(1)}, u32[]{:S(2)}, u32[]{:S(2)}) collective-permute-start(f32[96,768]{1,0:T(8,128)S(1)} %collective-permute-done), channel_id=1, source_target_pairs={{0,16},{1,17},{2,18},{3,19},{4,20},{5,21},{6,22},{7,23},{8,24},{9,... | collective-permute-start | bytes 884744 | tf_op jit(solution)/shard_map/ppermute | solution.py:60
  29.1 35.3 %collective-permute-start.2 = (f32[96,768]{1,0:T(8,128)S(1)}, f32[96,768]{1,0:T(8,128)S(1)}, u32[]{:S(2)}, u32[]{:S(2)}) collective-permute-start(f32[96,768]{1,0:T(8,128)S(1)} %collective-permute-done), channel_id=1, source_target_pairs={{0,32},{1,33},{2,34},{3,35},{4,36},{5,37},{6,38},{7,39},{8,40},{9,... | collective-permute-start | bytes 884744 | tf_op jit(solution)/shard_map/ppermute | solution.py:60
  33.7 30.7 %collective-permute-start.3 = (f32[96,768]{1,0:T(8,128)S(1)}, f32[96,768]{1,0:T(8,128)S(1)}, u32[]{:S(2)}, u32[]{:S(2)}) collective-permute-start(f32[96,768]{1,0:T(8,128)S(1)} %collective-permute-done), channel_id=1, source_target_pairs={{0,48},{1,49},{2,50},{3,51},{4,52},{5,53},{6,54},{7,55},{8,56},{9,... | collective-permute-start | bytes 884744 | tf_op jit(solution)/shard_map/ppermute | solution.py:60
  43.1 26.4 %copy-start.3 = (s32[2,16]{1,0:T(2,128)S(1)}, s32[2,16]{1,0:T(2,128)}, u32[]{:S(2)}) copy-start(s32[2,16]{1,0:T(2,128)} %param.6) | copy-start | bytes 388
  64.5 16.4 %collective-permute-start.4 = (f32[192,768]{1,0:T(8,128)S(1)}, f32[192,768]{1,0:T(8,128)S(1)}, u32[]{:S(2)}, u32[]{:S(2)}) collective-permute-start(f32[192,768]{1,0:T(8,128)S(1)} %pad_maximum_fusion.refs_0_), channel_id=1, source_target_pairs={{0,192},{1,193},{2,194},{3,195},{4,196},{5,197},{6,198},{7,199},{8... | collective-permute-start | bytes 1769480 | tf_op jit(solution)/shard_map/ppermute | solution.py:60
  67.0 22.4 %collective-permute-start.5 = (f32[192,768]{1,0:T(8,128)S(1)}, f32[192,768]{1,0:T(8,128)S(1)}, u32[]{:S(2)}, u32[]{:S(2)}) collective-permute-start(f32[192,768]{1,0:T(8,128)S(1)} %pad_maximum_fusion.refs_0_), channel_id=1, source_target_pairs={{0,128},{1,129},{2,130},{3,131},{4,132},{5,133},{6,134},{7,135},{8... | collective-permute-start | bytes 1769480 | tf_op jit(solution)/shard_map/ppermute | solution.py:60
  67.0 26.2 %collective-permute-start.6 = (f32[192,768]{1,0:T(8,128)S(1)}, f32[192,768]{1,0:T(8,128)S(1)}, u32[]{:S(2)}, u32[]{:S(2)}) collective-permute-start(f32[192,768]{1,0:T(8,128)S(1)} %pad_maximum_fusion.refs_0_), channel_id=1, source_target_pairs={{0,64},{1,65},{2,66},{3,67},{4,68},{5,69},{6,70},{7,71},{8,72},{9,... | collective-permute-start | bytes 1769480 | tf_op jit(solution)/shard_map/ppermute | solution.py:60
  72.3 1.7 copy-start.1
  74.0 1.7 copy-start.2
  93.2 20.3 %collective-permute-start.10 = (f32[192,768]{1,0:T(8,128)S(1)}, f32[192,768]{1,0:T(8,128)S(1)}, u32[]{:S(2)}, u32[]{:S(2)}) collective-permute-start(f32[192,768]{1,0:T(8,128)S(1)} %pad_maximum_fusion.1.refs_0_), channel_id=1, source_target_pairs={{0,64},{1,65},{2,66},{3,67},{4,68},{5,69},{6,70},{7,71},{8,72},{9,... | collective-permute-start | bytes 1769480 | tf_op jit(solution)/shard_map/ppermute | solution.py:60
  102.1 37.1 %collective-permute-start.7 = (f32[384,384]{1,0:T(8,128)S(1)}, f32[384,384]{1,0:T(8,128)S(1)}, u32[]{:S(2)}, u32[]{:S(2)}) collective-permute-start(f32[384,384]{1,0:T(8,128)S(1)} %get-tuple-element.27), channel_id=1, source_target_pairs={{0,0},{18,1},{1,2},{2,3},{49,4},{22,5},{7,6},{6,7},{9,8},{10,9},{2... | collective-permute-start | bytes 1769480 | tf_op jit(solution)/shard_map/ppermute | solution.py:117
  111.4 34.2 %collective-permute-start.8 = (f32[192,768]{1,0:T(8,128)S(1)}, f32[192,768]{1,0:T(8,128)S(1)}, u32[]{:S(2)}, u32[]{:S(2)}) collective-permute-start(f32[192,768]{1,0:T(8,128)S(1)} %pad_maximum_fusion.1.refs_0_), channel_id=1, source_target_pairs={{0,192},{1,193},{2,194},{3,195},{4,196},{5,197},{6,198},{7,199},{8... | collective-permute-start | bytes 1769480 | tf_op jit(solution)/shard_map/ppermute | solution.py:60
  111.5 34.2 %collective-permute-start.9 = (f32[192,768]{1,0:T(8,128)S(1)}, f32[192,768]{1,0:T(8,128)S(1)}, u32[]{:S(2)}, u32[]{:S(2)}) collective-permute-start(f32[192,768]{1,0:T(8,128)S(1)} %pad_maximum_fusion.1.refs_0_), channel_id=1, source_target_pairs={{0,128},{1,129},{2,130},{3,131},{4,132},{5,133},{6,134},{7,135},{8... | collective-permute-start | bytes 1769480 | tf_op jit(solution)/shard_map/ppermute | solution.py:60
  111.6 36.6 %collective-permute-start.11 = (f32[384,384]{1,0:T(8,128)}, f32[384,384]{1,0:T(8,128)S(1)}, u32[]{:S(2)}, u32[]{:S(2)}) collective-permute-start(f32[384,384]{1,0:T(8,128)} %get-tuple-element.34), channel_id=1, source_target_pairs={{17,0},{1,1},{19,2},{64,3},{5,4},{65,5},{113,6},{24,7},{25,8},{8,9... | collective-permute-start | bytes 1769480 | tf_op jit(solution)/shard_map/ppermute | solution.py:117
  113.5 42.6 %collective-permute-start.12 = (f32[384,384]{1,0:T(8,128)}, f32[384,384]{1,0:T(8,128)}, u32[]{:S(2)}, u32[]{:S(2)}) collective-permute-start(f32[384,384]{1,0:T(8,128)} %get-tuple-element.35), channel_id=1, source_target_pairs={{1,0},{2,1},{48,2},{20,3},{21,4},{64,5},{5,6},{8,7},{7,8},{26,9},{... | collective-permute-start | bytes 1769480 | tf_op jit(solution)/shard_map/ppermute | solution.py:117
  139.2 23.5 %collective-permute-start.13 = (f32[384,384]{1,0:T(8,128)}, f32[384,384]{1,0:T(8,128)}, u32[]{:S(2)}, u32[]{:S(2)}) collective-permute-start(f32[384,384]{1,0:T(8,128)} %get-tuple-element.36), channel_id=1, source_target_pairs={{1,0},{0,1},{17,2},{18,3},{48,4},{6,5},{21,6},{22,7},{23,8},{129,9... | collective-permute-start | bytes 1769480 | tf_op jit(solution)/shard_map/ppermute | solution.py:117
  143.1 1.7 copy-start
  171.7 36.7 %collective-permute-start.14 = (f32[384,384]{1,0:T(8,128)S(1)}, f32[384,384]{1,0:T(8,128)S(1)}, u32[]{:S(2)}, u32[]{:S(2)}) collective-permute-start(f32[384,384]{1,0:T(8,128)S(1)} %get-tuple-element.37), channel_id=1, source_target_pairs={{0,0},{18,1},{1,2},{2,3},{49,4},{22,5},{7,6},{6,7},{9,8},{10,9},{2... | collective-permute-start | bytes 1769480 | tf_op jit(solution)/shard_map/ppermute | solution.py:117
  175.8 35.8 %collective-permute-start.15 = (f32[384,384]{1,0:T(8,128)S(1)}, f32[384,384]{1,0:T(8,128)S(1)}, u32[]{:S(2)}, u32[]{:S(2)}) collective-permute-start(f32[384,384]{1,0:T(8,128)S(1)} %get-tuple-element.38), channel_id=1, source_target_pairs={{17,0},{1,1},{19,2},{64,3},{5,4},{65,5},{113,6},{24,7},{25,8},{8,9... | collective-permute-start | bytes 1769480 | tf_op jit(solution)/shard_map/ppermute | solution.py:117
  179.1 55.9 %collective-permute-start.16 = (f32[384,384]{1,0:T(8,128)S(1)}, f32[384,384]{1,0:T(8,128)S(1)}, u32[]{:S(2)}, u32[]{:S(2)}) collective-permute-start(f32[384,384]{1,0:T(8,128)S(1)} %get-tuple-element.39), channel_id=1, source_target_pairs={{1,0},{2,1},{48,2},{20,3},{21,4},{64,5},{5,6},{8,7},{7,8},{26,9},{... | collective-permute-start | bytes 1769480 | tf_op jit(solution)/shard_map/ppermute | solution.py:117
  181.0 54.0 %collective-permute-start.17 = (f32[384,384]{1,0:T(8,128)S(1)}, f32[384,384]{1,0:T(8,128)S(1)}, u32[]{:S(2)}, u32[]{:S(2)}) collective-permute-start(f32[384,384]{1,0:T(8,128)S(1)} %get-tuple-element.40), channel_id=1, source_target_pairs={{1,0},{0,1},{17,2},{18,3},{48,4},{6,5},{21,6},{22,7},{23,8},{129,9... | collective-permute-start | bytes 1769480 | tf_op jit(solution)/shard_map/ppermute | solution.py:117
Sparse Core Ops, SparseCore 0:
  9.2 57.5 all-gather.6
  68.6 38.1 all-gather.4

commit v2 on v1

--- a/solution.py
+++ b/solution.py
@@ -13,40 +13,80 @@
 BF = jnp.bfloat16
 F32 = jnp.float32
 MIRRORED = (
-    0x001A2010015A8412,
-    0x92451A411A401A6D,
-    0x540354011481D4A1,
-    0x198A854AAD8A054C,
-    0x4450865A8076A858,
-    0x1A4912041A451045,
-    0x44211481542194A1,
-    0x20CAAC8A2548A580,
-    0x084B8056A9498812,
-    0x52491A4510451A08,
-    0x8081D4A190A1D421,
-    0xA5886548A5888504,
-    0x0CD2885AA058AC52,
-    0x1A4510451841108D,
-    0x54B1942504A194A1,
-    0x2108A120210A2100,
+    (
+        0x2018000204428412,
+        0x0A4100801A88126D,
+        0x50811080400044A1,
+        0x249881088D986748,
+        0x0408885A8852E850,
+        0x020C12081841100C,
+        0x4000440154814021,
+        0x2088AC880509B400,
+        0x081A88F2A8C28440,
+        0x12401C4508414004,
+        0xC00144A104218020,
+        0x81886708A1888180,
+        0x8C52A8C2A4580052,
+        0x1A41184100041805,
+        0xD0A10421402005A1,
+        0x2109A4002000A100,
+    ),
+    (
+        0x2018000204428412,
+        0x0A4100801A88126D,
+        0x50811080400044A1,
+        0x249881088D986748,
+        0x0408885A8852E850,
+        0x020C12081841100C,
+        0x4000440154814021,
+        0x2088AC880509B400,
+        0x081A88F2A8C28440,
+        0x12401C4508414004,
+        0xC00144A104218020,
+        0x81886708A1888180,
+        0x8C52A8C2A4580052,
+        0x1A41184100041805,
+        0xD0A10421402005A1,
+        0x2109A4002000A100,
+    ),
 )
 PERMUTATION = (
-    0x9C36C97893721B8D878DE1D24B2DB139,
-    0xB18D4B398778786C2D39396C1E6CD2E4,
-    0x3693D278C6B14E72E42D1E93871BE163,
-    0x4BB43927D21E1E2DC9728D2D4E366336,
-    0x1ED887E4E44E2D781B72B193931E2772,
-    0x396C2DE1782D4E93931B36E44E6CD89C,
-    0x634E2D391EB17836279C721BE46CD8C6,
-    0xC963D8E19C4B4BC963E4D827C9784B63,
-    0x6CB14B6C4B4B72D836636C8D4B3963C9,
-    0xC69C1E1E637272272DD2E42D4B3987D8,
-    0xB18D1E728DC6E11EC972D2274E27B478,
-    0xE163784B63C9D28DD84BC6E42DC94E87,
-    0x8D36D2D2391B9CE11E87B19C8DC6D2C6,
-    0x36B4B4781B87D89C4ED2D21B87392D1E,
-    0x72393678E4E11B1E399CC6722D1E2D39,
-    0x9C7887C9D24E9CB1399C1B9C39394BE1,
+    (
+        0x63C978874EE46C9339E49C1E1E2DD236,
+        0x6C4E1E6C6339396C4E78933627932739,
+        0xD86C2DC91B2DB4E16C1B1EB4874B7887,
+        0x4BC6871B636CC6B1D2781EE1B1C66C1B,
+        0x633636638787D86C2793781E36276CD2,
+        0x39632DB4D8B4279C274E637872C94E6C,
+        0xD293B44E27B472B41E63B43987D8394E,
+        0xC61BE49372722D276C934E788D63B18D,
+        0x4B2DE4B4D893B12D4E27D2D21E6C9C36,
+        0xD24E9CC62D72E4639C368D4EC94E6CC6,
+        0xB18D9C931EC9C96C93C9C64E8D7263C6,
+        0x1B3972939C9C87D263C6721BC6728D63,
+        0x4E7887D8D86C78361E2736D26C4EC939,
+        0xD8D8B139932DD21B2DE14EC6636C1BC9,
+        0xD86339B11E4EE44B4BE427C6781B2D6C,
+        0x634B63E47863394E4B3993B439C94E93,
+    ),
+    (
+        0x63C978874EE46C9339E49C1E1E2DD236,
+        0x6C4E1E6C6339396C4E78933627932739,
+        0xD86C2DC91B2DB4E16C1B1EB4874B7887,
+        0x4BC6871B636CC6B1D2781EE1B1C66C1B,
+        0x633636638787D86C2793781E36276CD2,
+        0x39632DB4D8B4279C274E637872C94E6C,
+        0xD293B44E27B472B41E63B43987D8394E,
+        0xC61BE49372722D276C934E788D63B18D,
+        0x4B2DE4B4D893B12D4E27D2D21E6C9C36,
+        0xD24E9CC62D72E4639C368D4EC94E6CC6,
+        0xB18D9C931EC9C96C93C9C64E8D7263C6,
+        0x1B3972939C9C87D263C6721BC6728D63,
+        0x4E7887D8D86C78361E2736D26C4EC939,
+        0xD8D8B139932DD21B2DE14EC6636C1BC9,
+        0xD86339B11E4EE44B4BE427C6781B2D6C,
+        0x634B63E47863394E4B3993B439C94E93,
+    ),
 )
 
 
@@ -87,14 +127,14 @@
 
 
 @functools.cache
-def quadrant_moves():
+def quadrant_moves(step):
     edges = [[] for _ in range(256)]
     for p in range(16):
         for q in range(16):
             for a in range(2):
                 for b in range(2):
                     source, sent = (swap(a, p), swap(b, q)), 2 * a + b
-                    flag = MIRRORED[p] >> (4 * q + sent) & 1
+                    flag = MIRRORED[step][p] >> (4 * q + sent) & 1
                     if flag:
                         source, sent = source[::-1], 2 * b + a
                     edges[16 * p + q].append((16 * source[0] + source[1], sent, 2 * a + b, flag))
@@ -102,7 +142,7 @@
     for device in range(256):
         p, q = divmod(device, 16)
         for source, sent, slot, flag in edges[device]:
-            m = PERMUTATION[p] >> (8 * q + 2 * slot) & 3
+            m = PERMUTATION[step][p] >> (8 * q + 2 * slot) & 3
             pairs[m].append((source, device))
             table[source, m] = sent
             table[device, 4 + m] = slot
@@ -112,9 +152,9 @@
     return pairs, table
 
 
-def move(quads):
+def move(step, quads):
     quads = lax.optimization_barrier(quads)
-    return [lax.ppermute(q, AXES, pairs) for q, pairs in zip(quads, quadrant_moves()[0])]
+    return [lax.ppermute(q, AXES, pairs) for q, pairs in zip(quads, quadrant_moves(step)[0])]
 
 
 def split(value):
@@ -150,20 +190,29 @@
     return jax.ShapeDtypeStruct(dims, dtype)
 
 
-def turn_factor(shift, factor):
+def row_slots(zl, shift):
+    return [
+        (4 * x + 2 * (zl ^ other) + c + shift) % 16
+        for x in range(4)
+        for c in range(2)
+        for other in range(2)
+    ]
+
+
+def turn_factor(slots, factor, piece):
     wide = factor.shape[1]
-    half = wide // 2
-    if not KERNELS:
-        return split(jnp.roll(factor, shift[0] * half, axis=0).T)
-
-    def kernel(shift_ref, factor_ref, high, low, whole):
-        at = pl.multiple_of(shift_ref[0] * half, half)
-        whole[pl.ds(at, half), :] = factor_ref[:half, :]
-        whole[pl.ds(half - at, half), :] = factor_ref[half:, :]
+    if not KERNELS:
+        order = jnp.zeros((16,), jnp.int32).at[slots].set(jnp.arange(16, dtype=jnp.int32))
+        return split(jnp.take(factor.reshape(16, piece, wide), order, axis=0).reshape(wide, wide).T)
+
+    def kernel(slots_ref, factor_ref, high, low, whole):
+        for n in range(wide // piece):
+            to = pl.ds(pl.multiple_of(slots_ref[n] * piece, 16), piece)
+            whole[to, :] = factor_ref[n * piece : (n + 1) * piece, :]
         high[...], low[...] = split(whole[...].T)
 
     outs = [shape((wide, wide), BF)] * 2
-    return call(kernel, outs, [shift, factor], 0, [pltpu.VMEM((wide, wide), F32)])
+    return call(kernel, outs, [slots, factor], 0, [pltpu.VMEM((wide, wide), F32)])
 
 
 def fill_factor(slots_ref, at, refs, piece, high, low):
@@ -320,10 +369,12 @@
     piece = rotations.shape[2]
     f = lax.axis_index("row")
     g = lax.axis_index("col")
-    y, zh = f // 4, f % 4
+    y, zh, zl = f // 4, f % 4, g // 2 % 2
     odd_f, odd_g = f % 2, g % 2
     far_first = jnp.where((odd_f == 1) | (f == 0), 1, 0)
-    table = lax.dynamic_index_in_dim(jnp.asarray(quadrant_moves()[1]), 16 * f + g, keepdims=False)
+    tables = np.concatenate([quadrant_moves(step)[1] for step in range(2)], axis=1)
+    table = lax.dynamic_index_in_dim(jnp.asarray(tables), 16 * f + g, keepdims=False)
+    table1, table2 = table[:12], table[12:]
 
     def vector(values):
         return jnp.stack([jnp.asarray(v, jnp.int32) for v in values])
@@ -333,20 +384,34 @@
         here = [lax.dynamic_index_in_dim(marks, i, keepdims=False) for i in (f, g)]
         return [here[0] ^ far_first, here[1] ^ jnp.where((odd_g == 1) | (g == 0), 1, 0)]
 
-    rows = [lax.all_gather(rotations[s, 0], "col", axis=0, tiled=True) for s in range(2)]
-    four = spread_z(turn_pieces(rotations.reshape(2 * piece, wide)))
-    col1 = spread_y(jnp.concatenate([v[:piece] for v in four], axis=0))
-    mine2 = jnp.concatenate([v[piece:] for v in four], axis=0)
-    middle = left(turn_factor(vector([0]), rows[0]), matrix)
+    pieces = rotations.reshape(2 * piece, wide)
+    turned = turn_pieces(pieces)
+    other = permute(pieces, lambda y, zh, x, zl, c: (y, zh, x, zl + 1, c))
+    other = after(other, turned)
+    lines = [[4 * x + 2 * l + c for x in range(4) for c in range(2)] for l in range(2)]
+    rows = [
+        lax.all_gather(
+            jnp.concatenate([v[s * piece : (s + 1) * piece] for v in (pieces, other)], axis=0),
+            "col",
+            axis=0,
+            tiled=True,
+            axis_index_groups=lines,
+        )
+        for s in range(2)
+    ]
+    col1 = spread_y(jnp.concatenate(spread_z(turned[:piece]), axis=0))
+    mine2 = jnp.concatenate(spread_z(turned[piece:]), axis=0)
+
+    middle = left(turn_factor(vector(row_slots(zl, 0)), rows[0], piece), matrix)
     col2 = spread_y(after(mine2, *col1[1:], middle[0]))
-    info1 = jnp.concatenate([table, vector(halves(0) + col_slots(y, zh, 0))])
-    moved = move(right(info1, middle, col1, piece))
-    turned = turn_factor(vector([1 - odd_f]), after(rows[1], moved[0]))
+    info1 = jnp.concatenate([table1, vector(halves(0) + col_slots(y, zh, 0))])
+    moved = move(0, right(info1, middle, col1, piece))
+    turned = turn_factor(vector(row_slots(zl, 8 - 8 * odd_f)), after(rows[1], moved[0]), piece)
     slots = vector(col_slots(y, zh, 8 - 8 * odd_g))
     factor = column_factor(slots, col2, piece)
-    info2 = jnp.concatenate([table, vector(halves(1))])
-    moved = move(both_sides(info2, turned, factor, moved))
-    return whole_block(table, moved, odd_f, odd_g)
+    info2 = jnp.concatenate([table2[:4], table1[4:], vector(halves(1))])
+    moved = move(1, both_sides(info2, turned, factor, moved))
+    return whole_block(table2, moved, odd_f, odd_g)
 
 
 def solution(mesh):

time: 245 us -> 241 us (0.984)
  the two profiles are of different devices: /device:TPU:121 before, /device:TPU:64 now
where the time goes in v2:
time: 241 us; the launch traced here: 240 us
  waiting for transfers between devices  99.4 us (41%)
  starting transfers between devices  87.5 us (36%)
  Pallas kernels  24.2 us (10%)
  between operations  16.8 us (7%)
  local copies, waits for them, and re-layouts  9.02 us (4%)
  other arithmetic  2.77 us (1%)
    ppermute x8, waiting for transfers between devices, move(): lax.ppermute(q, AXES, pairs)  55.2 us
    ppermute x8, starting transfers between devices, move(): lax.ppermute(q, AXES, pairs)  48.9 us
    ppermute x14, waiting for transfers between devices, permute(): return lax.ppermute(value, AXES, pairs)  44.1 us
    ppermute x14, starting transfers between devices, permute(): return lax.ppermute(value, AXES, pairs)  38.6 us
    pallas_call x7, Pallas kernels, call(): pl.pallas_call(kernel, out_shape=outs, in_specs=specs, out_specs=[pl.Bloc...  24.2 us
    unnamed x14, local copies, waits for them, and re-layouts  5.5 us
  transfers between devices with their start and end apart: 24, of which 10 were waited for; matrix products, arithmetic and copies ran while one was open for 2% of the time, Pallas kernels for 5%

profile of v2, /device:TPU:64, one launch (start us, length us, event | category | flops | bytes accessed | tf_op | source)
XLA Modules:
  0.0 239.6 jit_solution(2323726020936052572)
XLA Ops:
  8.5 4.6 %collective-permute-start = (f32[96,768]{1,0:T(8,128)}, f32[96,768]{1,0:T(8,128)S(1)}, u32[]{:S(2)}, u32[]{:S(2)}) collective-permute-start(f32[96,768]{1,0:T(8,128)} %bitcast.88), channel_id=1, source_target_pairs={{0,2},{1,3},{2,0},{3,1},{4,6},{5,7},{6,4},{7,5},{8,10},{9,11},{10,... | collective-permute-start | bytes 884744 | tf_op jit(solution)/shard_map/ppermute | solution.py:100
  15.8 8.2 %collective-permute-done = f32[96,768]{1,0:T(8,128)S(1)} collective-permute-done((f32[96,768]{1,0:T(8,128)}, f32[96,768]{1,0:T(8,128)S(1)}, u32[]{:S(2)}, u32[]{:S(2)}) %collective-permute-start) | collective-permute-done | bytes 294944 | tf_op jit(solution)/shard_map/ppermute | solution.py:100
  27.1 4.6 %collective-permute-start.3 = (f32[48,768]{1,0:T(8,128)S(1)}, f32[48,768]{1,0:T(8,128)S(1)}, u32[]{:S(2)}, u32[]{:S(2)}) collective-permute-start(f32[48,768]{1,0:T(8,128)S(1)} %get-tuple-element.44), channel_id=1, source_target_pairs={{0,32},{1,33},{2,34},{3,35},{4,36},{5,37},{6,38},{7,39},{8,40},{9,... | collective-permute-start | bytes 442376 | tf_op jit(solution)/shard_map/ppermute | solution.py:100
  32.9 5.9 %collective-permute-start.10 = (f32[48,768]{1,0:T(8,128)S(1)}, f32[48,768]{1,0:T(8,128)}, u32[]{:S(2)}, u32[]{:S(2)}) collective-permute-start(f32[48,768]{1,0:T(8,128)S(1)} %get-tuple-element.43), channel_id=1, source_target_pairs={{0,32},{1,33},{2,34},{3,35},{4,36},{5,37},{6,38},{7,39},{8,40},{9,... | collective-permute-start | bytes 442376 | tf_op jit(solution)/shard_map/ppermute | solution.py:100
  41.0 2.6 %collective-permute-done.2 = f32[48,768]{1,0:T(8,128)S(1)} collective-permute-done((f32[48,768]{1,0:T(8,128)S(1)}, f32[48,768]{1,0:T(8,128)S(1)}, u32[]{:S(2)}, u32[]{:S(2)}) %collective-permute-start.2) | collective-permute-done | bytes 147488 | tf_op jit(solution)/shard_map/ppermute | solution.py:100
  43.6 3.4 %collective-permute-start.9 = (f32[48,768]{1,0:T(8,128)S(1)}, f32[48,768]{1,0:T(8,128)}, u32[]{:S(2)}, u32[]{:S(2)}) collective-permute-start(f32[48,768]{1,0:T(8,128)S(1)} %get-tuple-element.43), channel_id=1, source_target_pairs={{0,16},{1,17},{2,18},{3,19},{4,20},{5,21},{6,22},{7,23},{8,24},{9,... | collective-permute-start | bytes 442376 | tf_op jit(solution)/shard_map/ppermute | solution.py:100
  47.0 6.8 %collective-permute-done.4 = f32[48,768]{1,0:T(8,128)S(1)} collective-permute-done((f32[48,768]{1,0:T(8,128)S(1)}, f32[48,768]{1,0:T(8,128)S(1)}, u32[]{:S(2)}, u32[]{:S(2)}) %collective-permute-start.4) | collective-permute-done | bytes 147488 | tf_op jit(solution)/shard_map/ppermute | solution.py:100
  53.9 8.3 %collective-permute-start.5 = (f32[192,768]{1,0:T(8,128)S(1)}, f32[192,768]{1,0:T(8,128)S(1)}, u32[]{:S(2)}, u32[]{:S(2)}) collective-permute-start(f32[192,768]{1,0:T(8,128)S(1)} %pad_maximum_fusion.refs_0_), channel_id=1, source_target_pairs={{0,192},{1,193},{2,194},{3,195},{4,196},{5,197},{6,198},{7,199},{8... | collective-permute-start | bytes 1769480 | tf_op jit(solution)/shard_map/ppermute | solution.py:100
  69.7 3.7 %shard_map.47 = (bf16[768,768]{1,0:T(8,128)(2,1)S(1)}, bf16[768,768]{1,0:T(8,128)(2,1)S(1)}) custom-call(s32[1]{0:T(128)} %constant.429.clone.1._, bf16[768,768]{1,0:T(8,128)(2,1)S(1)} %get-tuple-element.25.ah, bf16[768,768]{1,0:T(8,128)(2,1)S(1)} %get-tuple-element.26.al, f32[768,768]{1,0:T(8,128)S(1)} %copy-done.2), custom_call_target="tpu_custom_call" | custom-call | flops 2717908992 | bytes 7077892 | tf_op jit(solution)/shard_map/pallas_call | solution.py:178
  73.4 14.6 %collective-permute-done.5.refs_1_ = f32[192,768]{1,0:T(8,128)S(1)} collective-permute-done((f32[192,768]{1,0:T(8,128)S(1)}, f32[192,768]{1,0:T(8,128)S(1)}, u32[]{:S(2)}, u32[]{:S(2)}) %collective-permute-start.5) | collective-permute-done | bytes 589856 | tf_op jit(solution)/shard_map/ppermute | solution.py:100
  88.0 3.7 %collective-permute-done.7.refs_3_ = f32[192,768]{1,0:T(8,128)S(1)} collective-permute-done((f32[192,768]{1,0:T(8,128)S(1)}, f32[192,768]{1,0:T(8,128)S(1)}, u32[]{:S(2)}, u32[]{:S(2)}) %collective-permute-start.7) | collective-permute-done | bytes 589856 | tf_op jit(solution)/shard_map/ppermute | solution.py:100
  94.2 4.7 %shard_map.48 = (f32[384,384]{1,0:T(8,128)S(1)}, f32[384,384]{1,0:T(8,128)}, f32[384,384]{1,0:T(8,128)}, f32[384,384]{1,0:T(8,128)S(1)}) custom-call(s32[30]{0:T(128)S(1)} %concatenate.24.info_ref, bf16[768,768]{1,0:T(8,128)(2,1)S(1)} %get-tuple-element.27.th, bf16[768,768]{1,0:T(8,128)(2,1)S(1)} %get-tuple-element.28.tl, ...), custom_call_target="tpu_custom_call" | custom-call | flops 2717908992 | bytes 7078008 | tf_op jit(solution)/shard_map/pallas_call | solution.py:178
  101.9 3.6 %collective-permute-start.14 = (f32[192,768]{1,0:T(8,128)S(1)}, f32[192,768]{1,0:T(8,128)S(1)}, u32[]{:S(2)}, u32[]{:S(2)}) collective-permute-start(f32[192,768]{1,0:T(8,128)S(1)} %pad_maximum_fusion.1.refs_0_), channel_id=1, source_target_pairs={{0,64},{1,65},{2,66},{3,67},{4,68},{5,69},{6,70},{7,71},{8,72},{9,... | collective-permute-start | bytes 1769480 | tf_op jit(solution)/shard_map/ppermute | solution.py:100
  105.5 6.0 %collective-permute-start.15 = (f32[384,384]{1,0:T(8,128)}, f32[384,384]{1,0:T(8,128)}, u32[]{:S(2)}, u32[]{:S(2)}) collective-permute-start(f32[384,384]{1,0:T(8,128)} %get-tuple-element.36), channel_id=1, source_target_pairs={{1,0},{0,1},{19,2},{2,3},{5,4},{64,5},{21,6},{22,7},{9,8},{10,9},{... | collective-permute-start | bytes 1769480 | tf_op jit(solution)/shard_map/ppermute | solution.py:157
  111.5 20.4 %collective-permute-start.16 = (f32[384,384]{1,0:T(8,128)}, f32[384,384]{1,0:T(8,128)}, u32[]{:S(2)}, u32[]{:S(2)}) collective-permute-start(f32[384,384]{1,0:T(8,128)} %get-tuple-element.37), channel_id=1, source_target_pairs={{17,0},{1,1},{48,2},{18,3},{21,4},{6,5},{112,6},{24,7},{7,8},{8,9}... | collective-permute-start | bytes 1769480 | tf_op jit(solution)/shard_map/ppermute | solution.py:157
  131.9 1.9 collective-permute-start.17
  139.2 6.4 %collective-permute-done.14.refs_3_ = f32[192,768]{1,0:T(8,128)S(1)} collective-permute-done((f32[192,768]{1,0:T(8,128)S(1)}, f32[192,768]{1,0:T(8,128)S(1)}, u32[]{:S(2)}, u32[]{:S(2)}) %collective-permute-start.14) | collective-permute-done | bytes 589856 | tf_op jit(solution)/shard_map/ppermute | solution.py:100
  146.5 11.2 %collective-permute-done.17.refs_3_ = f32[384,384]{1,0:T(8,128)} collective-permute-done((f32[384,384]{1,0:T(8,128)S(1)}, f32[384,384]{1,0:T(8,128)}, u32[]{:S(2)}, u32[]{:S(2)}) %collective-permute-start.17) | collective-permute-done | bytes 589856 | tf_op jit(solution)/shard_map/ppermute | solution.py:157
  157.7 9.5 %shard_map.51 = (f32[384,384]{1,0:T(8,128)S(1)}, f32[384,384]{1,0:T(8,128)S(1)}, f32[384,384]{1,0:T(8,128)S(1)}, f32[384,384]{1,0:T(8,128)S(1)}) custom-call(s32[14]{0:T(128)S(1)} %pad_add_fusion.1.info_ref, bf16[768,768]{1,0:T(8,128)(2,1)S(1)} %get-tuple-element.31.ah, bf16[768,768]{1,0:T(8,128)(2,1)S(1)} %get-tuple-element.32.al, ...), custom_call_target="tpu_custom_call" | custom-call | flops 5435817984 | bytes 9437240 | tf_op jit(solution)/shard_map/pallas_call | solution.py:178
  169.8 11.5 %collective-permute-start.20 = (f32[384,384]{1,0:T(8,128)S(1)}, f32[384,384]{1,0:T(8,128)S(1)}, u32[]{:S(2)}, u32[]{:S(2)}) collective-permute-start(f32[384,384]{1,0:T(8,128)S(1)} %get-tuple-element.41), channel_id=1, source_target_pairs={{17,0},{1,1},{48,2},{18,3},{21,4},{6,5},{112,6},{24,7},{7,8},{8,9}... | collective-permute-start | bytes 1769480 | tf_op jit(solution)/shard_map/ppermute | solution.py:157
  181.3 4.6 %collective-permute-start.21 = (f32[384,384]{1,0:T(8,128)S(1)}, f32[384,384]{1,0:T(8,128)S(1)}, u32[]{:S(2)}, u32[]{:S(2)}) collective-permute-start(f32[384,384]{1,0:T(8,128)S(1)} %get-tuple-element.42), channel_id=1, source_target_pairs={{1,0},{2,1},{17,2},{20,3},{49,4},{22,5},{5,6},{6,7},{25,8},{26,9},... | collective-permute-start | bytes 1769480 | tf_op jit(solution)/shard_map/ppermute | solution.py:157
  186.0 19.4 %collective-permute-done.18.refs_0_ = f32[384,384]{1,0:T(8,128)S(1)} collective-permute-done((f32[384,384]{1,0:T(8,128)S(1)}, f32[384,384]{1,0:T(8,128)S(1)}, u32[]{:S(2)}, u32[]{:S(2)}) %collective-permute-start.18) | collective-permute-done | bytes 589856 | tf_op jit(solution)/shard_map/ppermute | solution.py:157
  205.4 24.6 %collective-permute-done.21.refs_3_ = f32[384,384]{1,0:T(8,128)S(1)} collective-permute-done((f32[384,384]{1,0:T(8,128)S(1)}, f32[384,384]{1,0:T(8,128)S(1)}, u32[]{:S(2)}, u32[]{:S(2)}) %collective-permute-start.21) | collective-permute-done | bytes 589856 | tf_op jit(solution)/shard_map/ppermute | solution.py:157
  230.1 2.7 %shard_map.52 = f32[768,768]{1,0:T(8,128)} custom-call(s32[14]{0:T(128)S(1)} %pad_add_fusion.info_ref, f32[384,384]{1,0:T(8,128)S(1)} %collective-permute-done.18.refs_0_, f32[384,384]{1,0:T(8,128)S(1)} %collective-permute-done.19.refs_1_, f32[384,384]{1,0:T(8,128)S(1)} %collective-permute-done.20.refs_2_, f32[384,384]{1,0:T(8,128)S(1)} %collective-permute-done.21.refs_3_), custom_call_target="tpu_custom_call" | custom-call | bytes 4718648 | tf_op jit(solution)/shard_map/pallas_call | solution.py:178
  (66 shorter events, 29.9 us)
Async XLA Ops:
  6.5 59.8 %all-gather.5.cloned.1.call-start = ((), (), s32[]{:S(2)}) async-start(), calls=%async_computation.1 | async-start | bytes 2654208 | tf_op jit(solution)/shard_map/all_gather | solution.py:393
  6.5 9.2 %collective-permute-start.1 = (f32[96,768]{1,0:T(8,128)}, f32[96,768]{1,0:T(8,128)S(1)}, u32[]{:S(2)}, u32[]{:S(2)}) collective-permute-start(f32[96,768]{1,0:T(8,128)} %bitcast.87), channel_id=1, source_target_pairs={{0,0},{1,16},{2,32},{3,48},{4,64},{5,80},{6,96},{7,112},{8,128},{9... | collective-permute-start | bytes 884744 | tf_op jit(solution)/shard_map/ppermute | solution.py:100
  8.5 15.5 %collective-permute-start = (f32[96,768]{1,0:T(8,128)}, f32[96,768]{1,0:T(8,128)S(1)}, u32[]{:S(2)}, u32[]{:S(2)}) collective-permute-start(f32[96,768]{1,0:T(8,128)} %bitcast.88), channel_id=1, source_target_pairs={{0,2},{1,3},{2,0},{3,1},{4,6},{5,7},{6,4},{7,5},{8,10},{9,11},{10,... | collective-permute-start | bytes 884744 | tf_op jit(solution)/shard_map/ppermute | solution.py:100
  24.8 111.4 %all-gather.3.cloned.1.call-start = ((), (), s32[]{:S(2)}) async-start(), calls=%async_computation | async-start | bytes 2654208 | tf_op jit(solution)/shard_map/all_gather | solution.py:393
  25.6 18.0 %collective-permute-start.2 = (f32[48,768]{1,0:T(8,128)S(1)}, f32[48,768]{1,0:T(8,128)S(1)}, u32[]{:S(2)}, u32[]{:S(2)}) collective-permute-start(f32[48,768]{1,0:T(8,128)S(1)} %get-tuple-element.44), channel_id=1, source_target_pairs={{0,16},{1,17},{2,18},{3,19},{4,20},{5,21},{6,22},{7,23},{8,24},{9,... | collective-permute-start | bytes 442376 | tf_op jit(solution)/shard_map/ppermute | solution.py:100
  27.1 19.9 %collective-permute-start.3 = (f32[48,768]{1,0:T(8,128)S(1)}, f32[48,768]{1,0:T(8,128)S(1)}, u32[]{:S(2)}, u32[]{:S(2)}) collective-permute-start(f32[48,768]{1,0:T(8,128)S(1)} %get-tuple-element.44), channel_id=1, source_target_pairs={{0,32},{1,33},{2,34},{3,35},{4,36},{5,37},{6,38},{7,39},{8,40},{9,... | collective-permute-start | bytes 442376 | tf_op jit(solution)/shard_map/ppermute | solution.py:100
  31.7 22.1 %collective-permute-start.4 = (f32[48,768]{1,0:T(8,128)S(1)}, f32[48,768]{1,0:T(8,128)S(1)}, u32[]{:S(2)}, u32[]{:S(2)}) collective-permute-start(f32[48,768]{1,0:T(8,128)S(1)} %get-tuple-element.44), channel_id=1, source_target_pairs={{0,48},{1,49},{2,50},{3,51},{4,52},{5,53},{6,54},{7,55},{8,56},{9,... | collective-permute-start | bytes 442376 | tf_op jit(solution)/shard_map/ppermute | solution.py:100
  32.9 30.3 %collective-permute-start.10 = (f32[48,768]{1,0:T(8,128)S(1)}, f32[48,768]{1,0:T(8,128)}, u32[]{:S(2)}, u32[]{:S(2)}) collective-permute-start(f32[48,768]{1,0:T(8,128)S(1)} %get-tuple-element.43), channel_id=1, source_target_pairs={{0,32},{1,33},{2,34},{3,35},{4,36},{5,37},{6,38},{7,39},{8,40},{9,... | collective-permute-start | bytes 442376 | tf_op jit(solution)/shard_map/ppermute | solution.py:100
  40.8 24.4 %collective-permute-start.11 = (f32[48,768]{1,0:T(8,128)S(1)}, f32[48,768]{1,0:T(8,128)}, u32[]{:S(2)}, u32[]{:S(2)}) collective-permute-start(f32[48,768]{1,0:T(8,128)S(1)} %get-tuple-element.43), channel_id=1, source_target_pairs={{0,48},{1,49},{2,50},{3,51},{4,52},{5,53},{6,54},{7,55},{8,56},{9,... | collective-permute-start | bytes 442376 | tf_op jit(solution)/shard_map/ppermute | solution.py:100
  43.6 21.6 %collective-permute-start.9 = (f32[48,768]{1,0:T(8,128)S(1)}, f32[48,768]{1,0:T(8,128)}, u32[]{:S(2)}, u32[]{:S(2)}) collective-permute-start(f32[48,768]{1,0:T(8,128)S(1)} %get-tuple-element.43), channel_id=1, source_target_pairs={{0,16},{1,17},{2,18},{3,19},{4,20},{5,21},{6,22},{7,23},{8,24},{9,... | collective-permute-start | bytes 442376 | tf_op jit(solution)/shard_map/ppermute | solution.py:100
  53.9 34.1 %collective-permute-start.5 = (f32[192,768]{1,0:T(8,128)S(1)}, f32[192,768]{1,0:T(8,128)S(1)}, u32[]{:S(2)}, u32[]{:S(2)}) collective-permute-start(f32[192,768]{1,0:T(8,128)S(1)} %pad_maximum_fusion.refs_0_), channel_id=1, source_target_pairs={{0,192},{1,193},{2,194},{3,195},{4,196},{5,197},{6,198},{7,199},{8... | collective-permute-start | bytes 1769480 | tf_op jit(solution)/shard_map/ppermute | solution.py:100
  62.1 25.8 %collective-permute-start.6 = (f32[192,768]{1,0:T(8,128)S(1)}, f32[192,768]{1,0:T(8,128)S(1)}, u32[]{:S(2)}, u32[]{:S(2)}) collective-permute-start(f32[192,768]{1,0:T(8,128)S(1)} %pad_maximum_fusion.refs_0_), channel_id=1, source_target_pairs={{0,128},{1,129},{2,130},{3,131},{4,132},{5,133},{6,134},{7,135},{8... | collective-permute-start | bytes 1769480 | tf_op jit(solution)/shard_map/ppermute | solution.py:100
  63.2 28.5 %collective-permute-start.7 = (f32[192,768]{1,0:T(8,128)S(1)}, f32[192,768]{1,0:T(8,128)S(1)}, u32[]{:S(2)}, u32[]{:S(2)}) collective-permute-start(f32[192,768]{1,0:T(8,128)S(1)} %pad_maximum_fusion.refs_0_), channel_id=1, source_target_pairs={{0,64},{1,65},{2,66},{3,67},{4,68},{5,69},{6,70},{7,71},{8,72},{9,... | collective-permute-start | bytes 1769480 | tf_op jit(solution)/shard_map/ppermute | solution.py:100
  92.5 19.0 %collective-permute-start.12 = (f32[192,768]{1,0:T(8,128)S(1)}, f32[192,768]{1,0:T(8,128)S(1)}, u32[]{:S(2)}, u32[]{:S(2)}) collective-permute-start(f32[192,768]{1,0:T(8,128)S(1)} %pad_maximum_fusion.1.refs_0_), channel_id=1, source_target_pairs={{0,192},{1,193},{2,194},{3,195},{4,196},{5,197},{6,198},{7,199},{8... | collective-permute-start | bytes 1769480 | tf_op jit(solution)/shard_map/ppermute | solution.py:100
  98.9 33.0 %collective-permute-start.8 = (f32[384,384]{1,0:T(8,128)S(1)}, f32[384,384]{1,0:T(8,128)S(1)}, u32[]{:S(2)}, u32[]{:S(2)}) collective-permute-start(f32[384,384]{1,0:T(8,128)S(1)} %get-tuple-element.29), channel_id=1, source_target_pairs={{0,0},{18,1},{1,2},{64,3},{3,4},{20,5},{23,6},{8,7},{113,8},{24,9}... | collective-permute-start | bytes 1769480 | tf_op jit(solution)/shard_map/ppermute | solution.py:157
  100.8 38.4 %collective-permute-start.13 = (f32[192,768]{1,0:T(8,128)S(1)}, f32[192,768]{1,0:T(8,128)S(1)}, u32[]{:S(2)}, u32[]{:S(2)}) collective-permute-start(f32[192,768]{1,0:T(8,128)S(1)} %pad_maximum_fusion.1.refs_0_), channel_id=1, source_target_pairs={{0,128},{1,129},{2,130},{3,131},{4,132},{5,133},{6,134},{7,135},{8... | collective-permute-start | bytes 1769480 | tf_op jit(solution)/shard_map/ppermute | solution.py:100
  101.9 43.8 %collective-permute-start.14 = (f32[192,768]{1,0:T(8,128)S(1)}, f32[192,768]{1,0:T(8,128)S(1)}, u32[]{:S(2)}, u32[]{:S(2)}) collective-permute-start(f32[192,768]{1,0:T(8,128)S(1)} %pad_maximum_fusion.1.refs_0_), channel_id=1, source_target_pairs={{0,64},{1,65},{2,66},{3,67},{4,68},{5,69},{6,70},{7,71},{8,72},{9,... | collective-permute-start | bytes 1769480 | tf_op jit(solution)/shard_map/ppermute | solution.py:100
  105.5 41.0 %collective-permute-start.15 = (f32[384,384]{1,0:T(8,128)}, f32[384,384]{1,0:T(8,128)}, u32[]{:S(2)}, u32[]{:S(2)}) collective-permute-start(f32[384,384]{1,0:T(8,128)} %get-tuple-element.36), channel_id=1, source_target_pairs={{1,0},{0,1},{19,2},{2,3},{5,4},{64,5},{21,6},{22,7},{9,8},{10,9},{... | collective-permute-start | bytes 1769480 | tf_op jit(solution)/shard_map/ppermute | solution.py:157
  111.5 35.0 %collective-permute-start.16 = (f32[384,384]{1,0:T(8,128)}, f32[384,384]{1,0:T(8,128)}, u32[]{:S(2)}, u32[]{:S(2)}) collective-permute-start(f32[384,384]{1,0:T(8,128)} %get-tuple-element.37), channel_id=1, source_target_pairs={{17,0},{1,1},{48,2},{18,3},{21,4},{6,5},{112,6},{24,7},{7,8},{8,9}... | collective-permute-start | bytes 1769480 | tf_op jit(solution)/shard_map/ppermute | solution.py:157
  131.9 25.8 %collective-permute-start.17 = (f32[384,384]{1,0:T(8,128)S(1)}, f32[384,384]{1,0:T(8,128)}, u32[]{:S(2)}, u32[]{:S(2)}) collective-permute-start(f32[384,384]{1,0:T(8,128)S(1)} %get-tuple-element.38), channel_id=1, source_target_pairs={{1,0},{2,1},{17,2},{20,3},{49,4},{22,5},{5,6},{6,7},{25,8},{26,9},... | collective-permute-start | bytes 1769480 | tf_op jit(solution)/shard_map/ppermute | solution.py:157
  167.2 38.3 %collective-permute-start.18 = (f32[384,384]{1,0:T(8,128)S(1)}, f32[384,384]{1,0:T(8,128)S(1)}, u32[]{:S(2)}, u32[]{:S(2)}) collective-permute-start(f32[384,384]{1,0:T(8,128)S(1)} %get-tuple-element.39), channel_id=1, source_target_pairs={{0,0},{18,1},{1,2},{64,3},{3,4},{20,5},{23,6},{8,7},{113,8},{24,9}... | collective-permute-start | bytes 1769480 | tf_op jit(solution)/shard_map/ppermute | solution.py:157
  169.1 36.3 %collective-permute-start.19 = (f32[384,384]{1,0:T(8,128)S(1)}, f32[384,384]{1,0:T(8,128)S(1)}, u32[]{:S(2)}, u32[]{:S(2)}) collective-permute-start(f32[384,384]{1,0:T(8,128)S(1)} %get-tuple-element.40), channel_id=1, source_target_pairs={{1,0},{0,1},{19,2},{2,3},{5,4},{64,5},{21,6},{22,7},{9,8},{10,9},{... | collective-permute-start | bytes 1769480 | tf_op jit(solution)/shard_map/ppermute | solution.py:157
  169.8 35.6 %collective-permute-start.20 = (f32[384,384]{1,0:T(8,128)S(1)}, f32[384,384]{1,0:T(8,128)S(1)}, u32[]{:S(2)}, u32[]{:S(2)}) collective-permute-start(f32[384,384]{1,0:T(8,128)S(1)} %get-tuple-element.41), channel_id=1, source_target_pairs={{17,0},{1,1},{48,2},{18,3},{21,4},{6,5},{112,6},{24,7},{7,8},{8,9}... | collective-permute-start | bytes 1769480 | tf_op jit(solution)/shard_map/ppermute | solution.py:157
  181.3 48.7 %collective-permute-start.21 = (f32[384,384]{1,0:T(8,128)S(1)}, f32[384,384]{1,0:T(8,128)S(1)}, u32[]{:S(2)}, u32[]{:S(2)}) collective-permute-start(f32[384,384]{1,0:T(8,128)S(1)} %get-tuple-element.42), channel_id=1, source_target_pairs={{1,0},{2,1},{17,2},{20,3},{49,4},{22,5},{5,6},{6,7},{25,8},{26,9},... | collective-permute-start | bytes 1769480 | tf_op jit(solution)/shard_map/ppermute | solution.py:157
  (7 other events, 43.3 us)
Sparse Core Ops, SparseCore 0:
  24.9 33.8 all-gather.4
  60.6 28.7 all-gather.2

commit v3 on v2

--- a/solution.py
+++ b/solution.py
@@ -32,22 +32,22 @@
         0x2109A4002000A100,
     ),
     (
-        0x2018000204428412,
-        0x0A4100801A88126D,
-        0x50811080400044A1,
-        0x249881088D986748,
-        0x0408885A8852E850,
-        0x020C12081841100C,
-        0x4000440154814021,
-        0x2088AC880509B400,
-        0x081A88F2A8C28440,
-        0x12401C4508414004,
-        0xC00144A104218020,
-        0x81886708A1888180,
-        0x8C52A8C2A4580052,
-        0x1A41184100041805,
-        0xD0A10421402005A1,
-        0x2109A4002000A100,
+        0x0812A012001A8012,
+        0x1A491A401A491B6D,
+        0x1C811481540154A1,
+        0xA18A850A85082588,
+        0x80188C5A8050885A,
+        0x1A401A491A45100D,
+        0xC021148154A194A1,
+        0x2008850805088500,
+        0x00588050885AA810,
+        0x1A491A4512441244,
+        0x540154E1148114A1,
+        0xA08A054805400508,
+        0x4C52A0D8A0588C93,
+        0x1A4D10451A401245,
+        0x54A11481442114A9,
+        0x2100A5000108A100,
     ),
 )
 PERMUTATION = (
@@ -70,22 +70,22 @@
         0x634B63E47863394E4B3993B439C94E93,
     ),
     (
-        0x63C978874EE46C9339E49C1E1E2DD236,
-        0x6C4E1E6C6339396C4E78933627932739,
-        0xD86C2DC91B2DB4E16C1B1EB4874B7887,
-        0x4BC6871B636CC6B1D2781EE1B1C66C1B,
-        0x633636638787D86C2793781E36276CD2,
-        0x39632DB4D8B4279C274E637872C94E6C,
-        0xD293B44E27B472B41E63B43987D8394E,
-        0xC61BE49372722D276C934E788D63B18D,
-        0x4B2DE4B4D893B12D4E27D2D21E6C9C36,
-        0xD24E9CC62D72E4639C368D4EC94E6CC6,
-        0xB18D9C931EC9C96C93C9C64E8D7263C6,
-        0x1B3972939C9C87D263C6721BC6728D63,
-        0x4E7887D8D86C78361E2736D26C4EC939,
-        0xD8D8B139932DD21B2DE14EC6636C1BC9,
-        0xD86339B11E4EE44B4BE427C6781B2D6C,
-        0x634B63E47863394E4B3993B439C94E93,
+        0x72B19C4B36E1721E8D1B78E11B2DE139,
+        0x724E272DD878399CB14E1E8DE48DC99C,
+        0x938D4BD8B4784EB18DD21E87C6B4E44B,
+        0xC99C399CD24E8D782DC9D82DE178B12D,
+        0x9C2DE4D24B939393879C78D2932DC96C,
+        0x4B6CE463B4728D931E1BC693E18D4EB4,
+        0xC66CD84EE48D78939C391B934BB1C69C,
+        0xD287E44B8DE1934EB46C784E874E63C9,
+        0x87B4C99C786C4EC6786C6CD24B78D227,
+        0x3636B1D8728D9C9C1ED2C9D2D827C993,
+        0xC99C78B4394B9C8D6C2DE1D26C3687D8,
+        0x9C1E36788DB1B18D4E78E1E4788D1B36,
+        0x4E721E87C64E8736E44BD86CD8B18D4E,
+        0x724E6CC9E46C27C9E193366372C6874B,
+        0x4E8D8DD8B12DB41E87C6D29C27E44B93,
+        0x1E6CB12DE1392D63E18D4EC9D8D8E46C,
     ),
 )
 

time: 241 us -> 239 us (level)
  the two profiles are of different devices: /device:TPU:64 before, /device:TPU:9 now
where the time goes in v3:
time: 239 us; the launch traced here: 238 us
  waiting for transfers between devices  93.1 us (39%)
  starting transfers between devices  92.5 us (39%)
  Pallas kernels  23.8 us (10%)
  between operations  17 us (7%)
  local copies, waits for them, and re-layouts  9.03 us (4%)
  other arithmetic  2.77 us (1%)
    ppermute x8, starting transfers between devices, move(): lax.ppermute(q, AXES, pairs)  61.4 us
    ppermute x14, waiting for transfers between devices, permute(): return lax.ppermute(value, AXES, pairs)  52 us
    ppermute x8, waiting for transfers between devices, move(): lax.ppermute(q, AXES, pairs)  41 us
    ppermute x14, starting transfers between devices, permute(): return lax.ppermute(value, AXES, pairs)  31 us
    pallas_call x7, Pallas kernels, call(): pl.pallas_call(kernel, out_shape=outs, in_specs=specs, out_specs=[pl.Bloc...  23.8 us
    unnamed x14, local copies, waits for them, and re-layouts  5.5 us
  transfers between devices with their start and end apart: 24, of which 12 were waited for; matrix products, arithmetic and copies ran while one was open for 2% of the time, Pallas kernels for 5%

profile of v3, /device:TPU:9, one launch (start us, length us, event | category | flops | bytes accessed | tf_op | source)
XLA Modules:
  0.0 238.2 jit_solution(8929609534740675411)
XLA Ops:
  6.5 6.3 %collective-permute-start.1 = (f32[96,768]{1,0:T(8,128)}, f32[96,768]{1,0:T(8,128)S(1)}, u32[]{:S(2)}, u32[]{:S(2)}) collective-permute-start(f32[96,768]{1,0:T(8,128)} %bitcast.87), channel_id=1, source_target_pairs={{0,0},{1,16},{2,32},{3,48},{4,64},{5,80},{6,96},{7,112},{8,128},{9... | collective-permute-start | bytes 884744 | tf_op jit(solution)/shard_map/ppermute | solution.py:100
  12.8 4.3 %collective-permute-start = (f32[96,768]{1,0:T(8,128)}, f32[96,768]{1,0:T(8,128)S(1)}, u32[]{:S(2)}, u32[]{:S(2)}) collective-permute-start(f32[96,768]{1,0:T(8,128)} %bitcast.88), channel_id=1, source_target_pairs={{0,2},{1,3},{2,0},{3,1},{4,6},{5,7},{6,4},{7,5},{8,10},{9,11},{10,... | collective-permute-start | bytes 884744 | tf_op jit(solution)/shard_map/ppermute | solution.py:100
  18.7 8.9 %collective-permute-done = f32[96,768]{1,0:T(8,128)S(1)} collective-permute-done((f32[96,768]{1,0:T(8,128)}, f32[96,768]{1,0:T(8,128)S(1)}, u32[]{:S(2)}, u32[]{:S(2)}) %collective-permute-start) | collective-permute-done | bytes 294944 | tf_op jit(solution)/shard_map/ppermute | solution.py:100
  29.8 5.8 %collective-permute-start.3 = (f32[48,768]{1,0:T(8,128)S(1)}, f32[48,768]{1,0:T(8,128)S(1)}, u32[]{:S(2)}, u32[]{:S(2)}) collective-permute-start(f32[48,768]{1,0:T(8,128)S(1)} %get-tuple-element.44), channel_id=1, source_target_pairs={{0,32},{1,33},{2,34},{3,35},{4,36},{5,37},{6,38},{7,39},{8,40},{9,... | collective-permute-start | bytes 442376 | tf_op jit(solution)/shard_map/ppermute | solution.py:100
  36.5 4.2 %collective-permute-start.10 = (f32[48,768]{1,0:T(8,128)S(1)}, f32[48,768]{1,0:T(8,128)}, u32[]{:S(2)}, u32[]{:S(2)}) collective-permute-start(f32[48,768]{1,0:T(8,128)S(1)} %get-tuple-element.43), channel_id=1, source_target_pairs={{0,32},{1,33},{2,34},{3,35},{4,36},{5,37},{6,38},{7,39},{8,40},{9,... | collective-permute-start | bytes 442376 | tf_op jit(solution)/shard_map/ppermute | solution.py:100
  42.8 5.5 %collective-permute-done.2 = f32[48,768]{1,0:T(8,128)S(1)} collective-permute-done((f32[48,768]{1,0:T(8,128)S(1)}, f32[48,768]{1,0:T(8,128)S(1)}, u32[]{:S(2)}, u32[]{:S(2)}) %collective-permute-start.2) | collective-permute-done | bytes 147488 | tf_op jit(solution)/shard_map/ppermute | solution.py:100
  48.4 8.0 %collective-permute-done.4 = f32[48,768]{1,0:T(8,128)S(1)} collective-permute-done((f32[48,768]{1,0:T(8,128)S(1)}, f32[48,768]{1,0:T(8,128)S(1)}, u32[]{:S(2)}, u32[]{:S(2)}) %collective-permute-start.4) | collective-permute-done | bytes 147488 | tf_op jit(solution)/shard_map/ppermute | solution.py:100
  56.5 4.2 %collective-permute-start.6 = (f32[192,768]{1,0:T(8,128)S(1)}, f32[192,768]{1,0:T(8,128)S(1)}, u32[]{:S(2)}, u32[]{:S(2)}) collective-permute-start(f32[192,768]{1,0:T(8,128)S(1)} %pad_maximum_fusion.refs_0_), channel_id=1, source_target_pairs={{0,128},{1,129},{2,130},{3,131},{4,132},{5,133},{6,134},{7,135},{8... | collective-permute-start | bytes 1769480 | tf_op jit(solution)/shard_map/ppermute | solution.py:100
  67.3 3.7 %shard_map.47 = (bf16[768,768]{1,0:T(8,128)(2,1)S(1)}, bf16[768,768]{1,0:T(8,128)(2,1)S(1)}) custom-call(s32[1]{0:T(128)} %constant.429.clone.1._, bf16[768,768]{1,0:T(8,128)(2,1)S(1)} %get-tuple-element.25.ah, bf16[768,768]{1,0:T(8,128)(2,1)S(1)} %get-tuple-element.26.al, f32[768,768]{1,0:T(8,128)S(1)} %copy-done.2), custom_call_target="tpu_custom_call" | custom-call | flops 2717908992 | bytes 7077892 | tf_op jit(solution)/shard_map/pallas_call | solution.py:178
  71.0 2.0 collective-permute-done.5.refs_1_
  73.0 13.6 %collective-permute-done.6.refs_2_ = f32[192,768]{1,0:T(8,128)S(1)} collective-permute-done((f32[192,768]{1,0:T(8,128)S(1)}, f32[192,768]{1,0:T(8,128)S(1)}, u32[]{:S(2)}, u32[]{:S(2)}) %collective-permute-start.6) | collective-permute-done | bytes 589856 | tf_op jit(solution)/shard_map/ppermute | solution.py:100
  88.3 2.8 %collective-permute-start.12 = (f32[192,768]{1,0:T(8,128)S(1)}, f32[192,768]{1,0:T(8,128)S(1)}, u32[]{:S(2)}, u32[]{:S(2)}) collective-permute-start(f32[192,768]{1,0:T(8,128)S(1)} %pad_maximum_fusion.1.refs_0_), channel_id=1, source_target_pairs={{0,192},{1,193},{2,194},{3,195},{4,196},{5,197},{6,198},{7,199},{8... | collective-permute-start | bytes 1769480 | tf_op jit(solution)/shard_map/ppermute | solution.py:100
  92.2 4.7 %shard_map.48 = (f32[384,384]{1,0:T(8,128)S(1)}, f32[384,384]{1,0:T(8,128)}, f32[384,384]{1,0:T(8,128)}, f32[384,384]{1,0:T(8,128)S(1)}) custom-call(s32[30]{0:T(128)S(1)} %concatenate.24.info_ref, bf16[768,768]{1,0:T(8,128)(2,1)S(1)} %get-tuple-element.27.th, bf16[768,768]{1,0:T(8,128)(2,1)S(1)} %get-tuple-element.28.tl, ...), custom_call_target="tpu_custom_call" | custom-call | flops 2717908992 | bytes 7078008 | tf_op jit(solution)/shard_map/pallas_call | solution.py:178
  96.9 7.3 %collective-permute-start.8 = (f32[384,384]{1,0:T(8,128)S(1)}, f32[384,384]{1,0:T(8,128)S(1)}, u32[]{:S(2)}, u32[]{:S(2)}) collective-permute-start(f32[384,384]{1,0:T(8,128)S(1)} %get-tuple-element.29), channel_id=1, source_target_pairs={{0,0},{18,1},{1,2},{64,3},{3,4},{20,5},{23,6},{8,7},{113,8},{24,9}... | collective-permute-start | bytes 1769480 | tf_op jit(solution)/shard_map/ppermute | solution.py:157
  105.4 2.2 collective-permute-start.15
  107.6 4.0 %collective-permute-start.16 = (f32[384,384]{1,0:T(8,128)}, f32[384,384]{1,0:T(8,128)}, u32[]{:S(2)}, u32[]{:S(2)}) collective-permute-start(f32[384,384]{1,0:T(8,128)} %get-tuple-element.37), channel_id=1, source_target_pairs={{17,0},{1,1},{48,2},{18,3},{21,4},{6,5},{112,6},{24,7},{7,8},{8,9}... | collective-permute-start | bytes 1769480 | tf_op jit(solution)/shard_map/ppermute | solution.py:157
  113.0 35.0 %collective-permute-start.17 = (f32[384,384]{1,0:T(8,128)S(1)}, f32[384,384]{1,0:T(8,128)}, u32[]{:S(2)}, u32[]{:S(2)}) collective-permute-start(f32[384,384]{1,0:T(8,128)S(1)} %get-tuple-element.38), channel_id=1, source_target_pairs={{1,0},{2,1},{17,2},{20,3},{49,4},{22,5},{5,6},{6,7},{25,8},{26,9},... | collective-permute-start | bytes 1769480 | tf_op jit(solution)/shard_map/ppermute | solution.py:157
  153.4 12.5 %collective-permute-done.14.refs_3_ = f32[192,768]{1,0:T(8,128)S(1)} collective-permute-done((f32[192,768]{1,0:T(8,128)S(1)}, f32[192,768]{1,0:T(8,128)S(1)}, u32[]{:S(2)}, u32[]{:S(2)}) %collective-permute-start.14) | collective-permute-done | bytes 589856 | tf_op jit(solution)/shard_map/ppermute | solution.py:100
  166.8 9.3 %shard_map.51 = (f32[384,384]{1,0:T(8,128)S(1)}, f32[384,384]{1,0:T(8,128)S(1)}, f32[384,384]{1,0:T(8,128)S(1)}, f32[384,384]{1,0:T(8,128)S(1)}) custom-call(s32[14]{0:T(128)S(1)} %pad_add_fusion.1.info_ref, bf16[768,768]{1,0:T(8,128)(2,1)S(1)} %get-tuple-element.31.ah, bf16[768,768]{1,0:T(8,128)(2,1)S(1)} %get-tuple-element.32.al, ...), custom_call_target="tpu_custom_call" | custom-call | flops 5435817984 | bytes 9437240 | tf_op jit(solution)/shard_map/pallas_call | solution.py:178
  176.1 1.9 collective-permute-start.18
  180.0 7.2 %collective-permute-start.20 = (f32[384,384]{1,0:T(8,128)S(1)}, f32[384,384]{1,0:T(8,128)S(1)}, u32[]{:S(2)}, u32[]{:S(2)}) collective-permute-start(f32[384,384]{1,0:T(8,128)S(1)} %get-tuple-element.41), channel_id=1, source_target_pairs={{1,0},{0,1},{3,2},{20,3},{5,4},{22,5},{21,6},{8,7},{25,8},{129,9},... | collective-permute-start | bytes 1769480 | tf_op jit(solution)/shard_map/ppermute | solution.py:157
  189.2 19.5 %collective-permute-done.18.refs_0_ = f32[384,384]{1,0:T(8,128)S(1)} collective-permute-done((f32[384,384]{1,0:T(8,128)S(1)}, f32[384,384]{1,0:T(8,128)S(1)}, u32[]{:S(2)}, u32[]{:S(2)}) %collective-permute-start.18) | collective-permute-done | bytes 589856 | tf_op jit(solution)/shard_map/ppermute | solution.py:157
  210.1 18.7 %collective-permute-done.21.refs_3_ = f32[384,384]{1,0:T(8,128)S(1)} collective-permute-done((f32[384,384]{1,0:T(8,128)S(1)}, f32[384,384]{1,0:T(8,128)S(1)}, u32[]{:S(2)}, u32[]{:S(2)}) %collective-permute-start.21) | collective-permute-done | bytes 589856 | tf_op jit(solution)/shard_map/ppermute | solution.py:157
  228.8 2.5 %shard_map.52 = f32[768,768]{1,0:T(8,128)} custom-call(s32[14]{0:T(128)S(1)} %pad_add_fusion.info_ref, f32[384,384]{1,0:T(8,128)S(1)} %collective-permute-done.18.refs_0_, f32[384,384]{1,0:T(8,128)S(1)} %collective-permute-done.19.refs_1_, f32[384,384]{1,0:T(8,128)S(1)} %collective-permute-done.20.refs_2_, f32[384,384]{1,0:T(8,128)S(1)} %collective-permute-done.21.refs_3_), custom_call_target="tpu_custom_call" | custom-call | bytes 4718648 | tf_op jit(solution)/shard_map/pallas_call | solution.py:178
  (66 shorter events, 27.1 us)
Async XLA Ops:
  6.5 57.4 %all-gather.5.cloned.1.call-start = ((), (), s32[]{:S(2)}) async-start(), calls=%async_computation.1 | async-start | bytes 2654208 | tf_op jit(solution)/shard_map/all_gather | solution.py:393
  6.5 12.2 %collective-permute-start.1 = (f32[96,768]{1,0:T(8,128)}, f32[96,768]{1,0:T(8,128)S(1)}, u32[]{:S(2)}, u32[]{:S(2)}) collective-permute-start(f32[96,768]{1,0:T(8,128)} %bitcast.87), channel_id=1, source_target_pairs={{0,0},{1,16},{2,32},{3,48},{4,64},{5,80},{6,96},{7,112},{8,128},{9... | collective-permute-start | bytes 884744 | tf_op jit(solution)/shard_map/ppermute | solution.py:100
  12.8 14.8 %collective-permute-start = (f32[96,768]{1,0:T(8,128)}, f32[96,768]{1,0:T(8,128)S(1)}, u32[]{:S(2)}, u32[]{:S(2)}) collective-permute-start(f32[96,768]{1,0:T(8,128)} %bitcast.88), channel_id=1, source_target_pairs={{0,2},{1,3},{2,0},{3,1},{4,6},{5,7},{6,4},{7,5},{8,10},{9,11},{10,... | collective-permute-start | bytes 884744 | tf_op jit(solution)/shard_map/ppermute | solution.py:100
  28.4 121.9 %all-gather.3.cloned.1.call-start = ((), (), s32[]{:S(2)}) async-start(), calls=%async_computation | async-start | bytes 2654208 | tf_op jit(solution)/shard_map/all_gather | solution.py:393
  29.3 19.1 %collective-permute-start.2 = (f32[48,768]{1,0:T(8,128)S(1)}, f32[48,768]{1,0:T(8,128)S(1)}, u32[]{:S(2)}, u32[]{:S(2)}) collective-permute-start(f32[48,768]{1,0:T(8,128)S(1)} %get-tuple-element.44), channel_id=1, source_target_pairs={{0,16},{1,17},{2,18},{3,19},{4,20},{5,21},{6,22},{7,23},{8,24},{9,... | collective-permute-start | bytes 442376 | tf_op jit(solution)/shard_map/ppermute | solution.py:100
  29.8 18.6 %collective-permute-start.3 = (f32[48,768]{1,0:T(8,128)S(1)}, f32[48,768]{1,0:T(8,128)S(1)}, u32[]{:S(2)}, u32[]{:S(2)}) collective-permute-start(f32[48,768]{1,0:T(8,128)S(1)} %get-tuple-element.44), channel_id=1, source_target_pairs={{0,32},{1,33},{2,34},{3,35},{4,36},{5,37},{6,38},{7,39},{8,40},{9,... | collective-permute-start | bytes 442376 | tf_op jit(solution)/shard_map/ppermute | solution.py:100
  35.6 20.8 %collective-permute-start.4 = (f32[48,768]{1,0:T(8,128)S(1)}, f32[48,768]{1,0:T(8,128)S(1)}, u32[]{:S(2)}, u32[]{:S(2)}) collective-permute-start(f32[48,768]{1,0:T(8,128)S(1)} %get-tuple-element.44), channel_id=1, source_target_pairs={{0,48},{1,49},{2,50},{3,51},{4,52},{5,53},{6,54},{7,55},{8,56},{9,... | collective-permute-start | bytes 442376 | tf_op jit(solution)/shard_map/ppermute | solution.py:100
  36.5 24.2 %collective-permute-start.10 = (f32[48,768]{1,0:T(8,128)S(1)}, f32[48,768]{1,0:T(8,128)}, u32[]{:S(2)}, u32[]{:S(2)}) collective-permute-start(f32[48,768]{1,0:T(8,128)S(1)} %get-tuple-element.43), channel_id=1, source_target_pairs={{0,32},{1,33},{2,34},{3,35},{4,36},{5,37},{6,38},{7,39},{8,40},{9,... | collective-permute-start | bytes 442376 | tf_op jit(solution)/shard_map/ppermute | solution.py:100
  42.6 20.2 %collective-permute-start.11 = (f32[48,768]{1,0:T(8,128)S(1)}, f32[48,768]{1,0:T(8,128)}, u32[]{:S(2)}, u32[]{:S(2)}) collective-permute-start(f32[48,768]{1,0:T(8,128)S(1)} %get-tuple-element.43), channel_id=1, source_target_pairs={{0,48},{1,49},{2,50},{3,51},{4,52},{5,53},{6,54},{7,55},{8,56},{9,... | collective-permute-start | bytes 442376 | tf_op jit(solution)/shard_map/ppermute | solution.py:100
  48.3 14.5 %collective-permute-start.9 = (f32[48,768]{1,0:T(8,128)S(1)}, f32[48,768]{1,0:T(8,128)}, u32[]{:S(2)}, u32[]{:S(2)}) collective-permute-start(f32[48,768]{1,0:T(8,128)S(1)} %get-tuple-element.43), channel_id=1, source_target_pairs={{0,16},{1,17},{2,18},{3,19},{4,20},{5,21},{6,22},{7,23},{8,24},{9,... | collective-permute-start | bytes 442376 | tf_op jit(solution)/shard_map/ppermute | solution.py:100
  56.4 16.6 %collective-permute-start.5 = (f32[192,768]{1,0:T(8,128)S(1)}, f32[192,768]{1,0:T(8,128)S(1)}, u32[]{:S(2)}, u32[]{:S(2)}) collective-permute-start(f32[192,768]{1,0:T(8,128)S(1)} %pad_maximum_fusion.refs_0_), channel_id=1, source_target_pairs={{0,192},{1,193},{2,194},{3,195},{4,196},{5,197},{6,198},{7,199},{8... | collective-permute-start | bytes 1769480 | tf_op jit(solution)/shard_map/ppermute | solution.py:100
  56.5 30.1 %collective-permute-start.6 = (f32[192,768]{1,0:T(8,128)S(1)}, f32[192,768]{1,0:T(8,128)S(1)}, u32[]{:S(2)}, u32[]{:S(2)}) collective-permute-start(f32[192,768]{1,0:T(8,128)S(1)} %pad_maximum_fusion.refs_0_), channel_id=1, source_target_pairs={{0,128},{1,129},{2,130},{3,131},{4,132},{5,133},{6,134},{7,135},{8... | collective-permute-start | bytes 1769480 | tf_op jit(solution)/shard_map/ppermute | solution.py:100
  60.7 26.8 %collective-permute-start.7 = (f32[192,768]{1,0:T(8,128)S(1)}, f32[192,768]{1,0:T(8,128)S(1)}, u32[]{:S(2)}, u32[]{:S(2)}) collective-permute-start(f32[192,768]{1,0:T(8,128)S(1)} %pad_maximum_fusion.refs_0_), channel_id=1, source_target_pairs={{0,64},{1,65},{2,66},{3,67},{4,68},{5,69},{6,70},{7,71},{8,72},{9,... | collective-permute-start | bytes 1769480 | tf_op jit(solution)/shard_map/ppermute | solution.py:100
  88.3 19.3 %collective-permute-start.12 = (f32[192,768]{1,0:T(8,128)S(1)}, f32[192,768]{1,0:T(8,128)S(1)}, u32[]{:S(2)}, u32[]{:S(2)}) collective-permute-start(f32[192,768]{1,0:T(8,128)S(1)} %pad_maximum_fusion.1.refs_0_), channel_id=1, source_target_pairs={{0,192},{1,193},{2,194},{3,195},{4,196},{5,197},{6,198},{7,199},{8... | collective-permute-start | bytes 1769480 | tf_op jit(solution)/shard_map/ppermute | solution.py:100
  96.9 16.1 %collective-permute-start.8 = (f32[384,384]{1,0:T(8,128)S(1)}, f32[384,384]{1,0:T(8,128)S(1)}, u32[]{:S(2)}, u32[]{:S(2)}) collective-permute-start(f32[384,384]{1,0:T(8,128)S(1)} %get-tuple-element.29), channel_id=1, source_target_pairs={{0,0},{18,1},{1,2},{64,3},{3,4},{20,5},{23,6},{8,7},{113,8},{24,9}... | collective-permute-start | bytes 1769480 | tf_op jit(solution)/shard_map/ppermute | solution.py:157
  104.2 49.2 %collective-permute-start.13 = (f32[192,768]{1,0:T(8,128)S(1)}, f32[192,768]{1,0:T(8,128)S(1)}, u32[]{:S(2)}, u32[]{:S(2)}) collective-permute-start(f32[192,768]{1,0:T(8,128)S(1)} %pad_maximum_fusion.1.refs_0_), channel_id=1, source_target_pairs={{0,128},{1,129},{2,130},{3,131},{4,132},{5,133},{6,134},{7,135},{8... | collective-permute-start | bytes 1769480 | tf_op jit(solution)/shard_map/ppermute | solution.py:100
  104.3 61.6 %collective-permute-start.14 = (f32[192,768]{1,0:T(8,128)S(1)}, f32[192,768]{1,0:T(8,128)S(1)}, u32[]{:S(2)}, u32[]{:S(2)}) collective-permute-start(f32[192,768]{1,0:T(8,128)S(1)} %pad_maximum_fusion.1.refs_0_), channel_id=1, source_target_pairs={{0,64},{1,65},{2,66},{3,67},{4,68},{5,69},{6,70},{7,71},{8,72},{9,... | collective-permute-start | bytes 1769480 | tf_op jit(solution)/shard_map/ppermute | solution.py:100
  105.4 61.4 %collective-permute-start.15 = (f32[384,384]{1,0:T(8,128)}, f32[384,384]{1,0:T(8,128)}, u32[]{:S(2)}, u32[]{:S(2)}) collective-permute-start(f32[384,384]{1,0:T(8,128)} %get-tuple-element.36), channel_id=1, source_target_pairs={{1,0},{0,1},{19,2},{2,3},{5,4},{64,5},{21,6},{22,7},{9,8},{10,9},{... | collective-permute-start | bytes 1769480 | tf_op jit(solution)/shard_map/ppermute | solution.py:157
  107.6 59.2 %collective-permute-start.16 = (f32[384,384]{1,0:T(8,128)}, f32[384,384]{1,0:T(8,128)}, u32[]{:S(2)}, u32[]{:S(2)}) collective-permute-start(f32[384,384]{1,0:T(8,128)} %get-tuple-element.37), channel_id=1, source_target_pairs={{17,0},{1,1},{48,2},{18,3},{21,4},{6,5},{112,6},{24,7},{7,8},{8,9}... | collective-permute-start | bytes 1769480 | tf_op jit(solution)/shard_map/ppermute | solution.py:157
  113.0 53.8 %collective-permute-start.17 = (f32[384,384]{1,0:T(8,128)S(1)}, f32[384,384]{1,0:T(8,128)}, u32[]{:S(2)}, u32[]{:S(2)}) collective-permute-start(f32[384,384]{1,0:T(8,128)S(1)} %get-tuple-element.38), channel_id=1, source_target_pairs={{1,0},{2,1},{17,2},{20,3},{49,4},{22,5},{5,6},{6,7},{25,8},{26,9},... | collective-permute-start | bytes 1769480 | tf_op jit(solution)/shard_map/ppermute | solution.py:157
  176.1 32.5 %collective-permute-start.18 = (f32[384,384]{1,0:T(8,128)S(1)}, f32[384,384]{1,0:T(8,128)S(1)}, u32[]{:S(2)}, u32[]{:S(2)}) collective-permute-start(f32[384,384]{1,0:T(8,128)S(1)} %get-tuple-element.39), channel_id=1, source_target_pairs={{0,0},{18,1},{1,2},{64,3},{49,4},{65,5},{5,6},{6,7},{7,8},{26,9},{... | collective-permute-start | bytes 1769480 | tf_op jit(solution)/shard_map/ppermute | solution.py:157
  178.1 30.6 %collective-permute-start.19 = (f32[384,384]{1,0:T(8,128)S(1)}, f32[384,384]{1,0:T(8,128)S(1)}, u32[]{:S(2)}, u32[]{:S(2)}) collective-permute-start(f32[384,384]{1,0:T(8,128)S(1)} %get-tuple-element.40), channel_id=1, source_target_pairs={{17,0},{1,1},{19,2},{2,3},{21,4},{6,5},{7,6},{22,7},{9,8},{10,9},{... | collective-permute-start | bytes 1769480 | tf_op jit(solution)/shard_map/ppermute | solution.py:157
  180.0 30.1 %collective-permute-start.20 = (f32[384,384]{1,0:T(8,128)S(1)}, f32[384,384]{1,0:T(8,128)S(1)}, u32[]{:S(2)}, u32[]{:S(2)}) collective-permute-start(f32[384,384]{1,0:T(8,128)S(1)} %get-tuple-element.41), channel_id=1, source_target_pairs={{1,0},{0,1},{3,2},{20,3},{5,4},{22,5},{21,6},{8,7},{25,8},{129,9},... | collective-permute-start | bytes 1769480 | tf_op jit(solution)/shard_map/ppermute | solution.py:157
  187.2 41.7 %collective-permute-start.21 = (f32[384,384]{1,0:T(8,128)S(1)}, f32[384,384]{1,0:T(8,128)S(1)}, u32[]{:S(2)}, u32[]{:S(2)}) collective-permute-start(f32[384,384]{1,0:T(8,128)S(1)} %get-tuple-element.42), channel_id=1, source_target_pairs={{1,0},{2,1},{17,2},{18,3},{48,4},{4,5},{23,6},{24,7},{113,8},{8,9}... | collective-permute-start | bytes 1769480 | tf_op jit(solution)/shard_map/ppermute | solution.py:157
  (7 other events, 37.1 us)
Sparse Core Ops, SparseCore 0:
  28.6 31.2 all-gather.4
  61.6 28.7 all-gather.2
